TPU v7x, 128 devices: a whole 4x4x4 slice. The times are simulated.
128 devices in a mesh: dp: 64 (over y, x, z_lo, core), tensor: 2 (over z_hi).
Axes of the slice: x: 4, y: 4, z: 4 (z_hi: 2, z_lo: 2; z = z_hi * 2 + z_lo), core: 2. Of those that a mesh axis runs over, the one named last changes fastest.
Arguments:
- block_input: bfloat16 [32768, 1536], P(('dp', 'tensor')), may hold values from -24 to 24
- cotangent: bfloat16 [32768, 1536], P(('dp', 'tensor')), may hold values from -24 to 24
- seg_ids: int32 [32768], P('dp'), may hold values from 0 to 6, as said below
- norm_gain: bfloat16 [1536], P(('dp', 'tensor')), may hold values from 0.25 to 1.75
- w_z: bfloat16 [1536, 3072], P('dp', 'tensor'), may hold values from -0.15625 to 0.15625
- w_x: bfloat16 [1536, 3072], P('dp', 'tensor'), may hold values from -0.15625 to 0.15625
- w_bc: bfloat16 [1536, 256], P(('dp', 'tensor')), may hold values from -0.15625 to 0.15625
- w_dt: bfloat16 [1536, 48], P('dp', 'tensor'), may hold values from -0.15625 to 0.15625
- conv_x_w: bfloat16 [4, 3072], P(None, 'tensor'), may hold values from -3 to 3
- conv_x_b: bfloat16 [3072], P('tensor'), may hold values from -3 to 3
- conv_bc_w: bfloat16 [4, 256], P(None, ('dp', 'tensor')), may hold values from -3 to 3
- conv_bc_b: bfloat16 [256], P(('dp', 'tensor')), may hold values from -3 to 3
- dt_bias: bfloat16 [48], P('tensor'), may hold values from -7 to -3
- a_log: bfloat16 [48], P('tensor'), may hold values from -1 to 1.5
- d_skip: bfloat16 [48], P('tensor'), may hold values from 0.5 to 1.5
- gate_gain: bfloat16 [3072], P('tensor'), may hold values from 0.25 to 1.75
- w_out: bfloat16 [3072, 1536], P('tensor', 'dp'), may hold values from -0.109375 to 0.109375
Outputs:
- out: bfloat16 [32768, 1536], P(('dp', 'tensor'))
- d_x: float32 [32768, 1536], P(('dp', 'tensor'))
- d_norm_gain: float32 [1536], P(('dp', 'tensor'))
- d_w_z: float32 [1536, 3072], P('dp', 'tensor')
- d_w_x: float32 [1536, 3072], P('dp', 'tensor')
- d_w_bc: float32 [1536, 256], P(('dp', 'tensor'))
- d_w_dt: float32 [1536, 48], P('dp', 'tensor')
- d_conv_x_w: float32 [4, 3072], P(None, 'tensor')
- d_conv_x_b: float32 [3072], P('tensor')
- d_conv_bc_w: float32 [4, 256], P(None, ('dp', 'tensor'))
- d_conv_bc_b: float32 [256], P(('dp', 'tensor'))
- d_dt_bias: float32 [48], P('tensor')
- d_a_log: float32 [48], P('tensor')
- d_d_skip: float32 [48], P('tensor')
- d_gate_gain: float32 [3072], P('tensor')
- d_w_out: float32 [3072, 1536], P('tensor', 'dp')
Inputs may be any that keep to these rules, and one draw needn't show every extreme that they name: `seg_ids`: ids never fall along each sequence of 512 tokens and begin at 0 in each; the tokens at positions 255 and 256 of every sequence share an id; a new document can begin only within the first 32 positions of each aligned run of 64 tokens; in one sequence a document begins in every such run but the one at 256.
All inputs are finite; a program needn't handle non-finite values.
Results may differ from a plain program's by a relative error of at most 0.0093.
Values may be sent and summed in bfloat16 or wider, within the bound.
A program may use at most 192 MiB of HBM per device.

v0:
```python
import jax
import jax.numpy as jnp
from jax import lax
from jax.sharding import PartitionSpec as P

CONV = 4
SCAN_BLOCK = 256


EPS = 1e-05


def silu_slope(values):
    sigma = jax.nn.sigmoid(values)
    return sigma * (1.0 + values * (1.0 - sigma))


def causal_conv(values, kernel, offsets, segments):
    length = values.shape[0]
    taps_count = kernel.shape[0]
    summed = offsets[None, :] + kernel[taps_count - 1][None, :] * values
    for distance in range(1, taps_count):
        shifted = jnp.pad(values, ((distance, 0), (0, 0)))[:length]
        same_doc = jnp.pad(segments, (distance, 0), constant_values=-1)[:length] == segments
        summed = summed + kernel[taps_count - 1 - distance][None, :] * shifted * same_doc[
            :, None
        ].astype(values.dtype)
    return summed


def conv_input_grad(extended, kernel, seg_ext):
    taps_count = kernel.shape[0]
    row_count = extended.shape[0] - (taps_count - 1)
    summed = jnp.zeros((row_count, extended.shape[1]), jnp.float32)
    for distance in range(taps_count):
        shifted = extended[distance : distance + row_count]
        same_doc = seg_ext[distance : distance + row_count] == seg_ext[:row_count]
        summed = summed + kernel[taps_count - 1 - distance][None, :] * shifted * same_doc[
            :, None
        ].astype(jnp.float32)
    return summed


def conv_kernel_grad(grad_rows, values, segments, row_start, row_count):
    length = values.shape[0]
    pieces = []
    distance = 0
    while distance < CONV:
        shifted = jnp.pad(values, ((distance, 0), (0, 0)))[:length]
        same_doc = jnp.pad(segments, (distance, 0), constant_values=-1)[:length] == segments
        masked = shifted * same_doc[:, None].astype(jnp.float32)
        window = lax.dynamic_slice_in_dim(masked, row_start, row_count, 0)
        pieces.append(jnp.sum(grad_rows * window, axis=0))
        distance = distance + 1
    return (jnp.stack(pieces[::-1]), jnp.sum(grad_rows, axis=0))


def state_space(inputs_x, bc_vals, dt_raw, dt_bias, a_log, d_skip, segments):
    length = inputs_x.shape[0]
    head_count = dt_bias.shape[0]
    head_dim = inputs_x.shape[1] // head_count
    state_size = bc_vals.shape[1] // 2
    block_count = length // SCAN_BLOCK
    highest = lax.Precision.HIGHEST
    step_size = jax.nn.softplus(dt_raw + dt_bias)
    log_decay = step_size * -jnp.exp(a_log)
    values = inputs_x.reshape(block_count, SCAN_BLOCK, head_count, head_dim)
    write_map = bc_vals[:, :state_size].reshape(block_count, SCAN_BLOCK, state_size)
    read_map = bc_vals[:, state_size:].reshape(block_count, SCAN_BLOCK, state_size)
    step_rows = step_size.reshape(block_count, SCAN_BLOCK, head_count).transpose(0, 2, 1)
    cumulative = jnp.cumsum(
        log_decay.reshape(block_count, SCAN_BLOCK, head_count), axis=1
    ).transpose(0, 2, 1)
    blocks = segments.reshape(block_count, SCAN_BLOCK)
    places = jnp.arange(SCAN_BLOCK)
    same_doc = (blocks[:, :, None] == blocks[:, None, :]) & (places[:, None] >= places[None, :])
    masked = same_doc[:, None]
    gap_sizes = cumulative[:, :, :, None] - cumulative[:, :, None, :]
    decays = jnp.where(masked, jnp.exp(jnp.where(masked, gap_sizes, 0.0)), 0.0)
    affinity = jnp.einsum("cin,cjn->cij", read_map, write_map, precision=highest)
    mixing = decays * affinity[:, None] * step_rows[:, :, None, :]
    within = jnp.einsum("chij,cjhp->cihp", mixing, values, precision=highest)
    finals = blocks[:, -1]
    tail_weight = (
        jnp.exp(cumulative[:, :, -1:] - cumulative)
        * (blocks == finals[:, None]).astype(values.dtype)[:, None, :]
        * step_rows
    )
    local_states = jnp.einsum(
        "chj,cjn,cjhp->chnp", tail_weight, write_map, values, precision=highest
    )
    earlier = jnp.concatenate([jnp.full((1,), -1, finals.dtype), finals[:-1]])
    carried = (finals == earlier).astype(values.dtype)
    through = jnp.exp(cumulative[:, :, -1]) * carried[:, None]

    def advance(entering, pieces):
        factor, fresh_state = pieces
        return (factor[:, None, None] * entering + fresh_state, entering)

    start_state = jnp.zeros(local_states.shape[1:], values.dtype)
    unused, entering = lax.scan(advance, start_state, (through, local_states))
    enters = (blocks == earlier[:, None]).astype(values.dtype)
    entry_decay = jnp.exp(cumulative).transpose(0, 2, 1) * enters[:, :, None]
    across = (
        jnp.einsum("cin,chnp->cihp", read_map, entering, precision=highest)
        * entry_decay[:, :, :, None]
    )
    mixed_out = (within + across).reshape(length, head_count * head_dim)
    return mixed_out + inputs_x * jnp.repeat(d_skip, head_dim)


def per_device(
    block_input,
    cotangent,
    seg_ids,
    norm_gain,
    w_z,
    w_x,
    w_bc,
    w_dt,
    conv_x_w,
    conv_x_b,
    conv_bc_w,
    conv_bc_b,
    dt_bias,
    a_log,
    d_skip,
    gate_gain,
    w_out,
):
    own_rows = block_input.shape[0]
    own_start = lax.axis_index("tensor") * own_rows
    taps_count = conv_x_w.shape[0]
    full_z, full_x, full_dt, full_out = (
        lax.all_gather(w_z, "dp", axis=0, tiled=True),
        lax.all_gather(w_x, "dp", axis=0, tiled=True),
        lax.all_gather(w_dt, "dp", axis=0, tiled=True),
        lax.all_gather(w_out, "dp", axis=1, tiled=True),
    )
    full_bc, full_gain, kern_bc, offset_bc = (
        lax.all_gather(w_bc, ("dp", "tensor"), axis=0, tiled=True),
        lax.all_gather(norm_gain, ("dp", "tensor"), axis=0, tiled=True),
        lax.all_gather(conv_bc_w, ("dp", "tensor"), axis=1, tiled=True),
        lax.all_gather(conv_bc_b, ("dp", "tensor"), axis=0, tiled=True),
    )
    inputs = block_input.astype(jnp.float32)
    inv_rms = lax.rsqrt(jnp.mean(inputs * inputs, axis=-1, keepdims=True) + EPS)
    unit_rows = inputs * inv_rms
    gain_in = full_gain.astype(jnp.float32)
    normed_own = (unit_rows * gain_in).astype(jnp.bfloat16)
    normed = lax.all_gather(normed_own, "tensor", axis=0, tiled=True)
    z_part = jnp.dot(normed, full_z, preferred_element_type=jnp.float32)
    x_pre = jnp.dot(normed, full_x, preferred_element_type=jnp.float32)
    bc_pre = jnp.dot(normed, full_bc, preferred_element_type=jnp.float32)
    dt_raw = jnp.dot(normed, full_dt, preferred_element_type=jnp.float32)
    kern_x = conv_x_w.astype(jnp.float32)
    kern_bcf = kern_bc.astype(jnp.float32)
    x_conv_pre = causal_conv(x_pre, kern_x, conv_x_b.astype(jnp.float32), seg_ids)
    bc_conv_pre = causal_conv(bc_pre, kern_bcf, offset_bc.astype(jnp.float32), seg_ids)
    x_conv = jax.nn.silu(x_conv_pre)
    bc_conv = jax.nn.silu(bc_conv_pre)

    def mixer_fn(values, bc_vals, raw_steps, bias_steps, log_rates, skip_gains):
        return state_space(values, bc_vals, raw_steps, bias_steps, log_rates, skip_gains, seg_ids)

    mixer, mixer_back = jax.vjp(
        mixer_fn,
        x_conv,
        bc_conv,
        dt_raw,
        dt_bias.astype(jnp.float32),
        a_log.astype(jnp.float32),
        d_skip.astype(jnp.float32),
    )
    gate_act = jax.nn.silu(z_part)
    gated = mixer * gate_act
    inner_width = gated.shape[1] * lax.axis_size("tensor")
    squares = lax.psum(jnp.sum(gated * gated, axis=-1), "tensor")
    inv_gate = lax.rsqrt(squares / inner_width + EPS)
    gain_gate = gate_gain.astype(jnp.float32)
    mixed = (gated * inv_gate[:, None] * gain_gate).astype(jnp.bfloat16)
    branch = lax.psum_scatter(
        jnp.dot(mixed, full_out, preferred_element_type=jnp.float32),
        "tensor",
        scatter_dimension=0,
        tiled=True,
    )
    out = (inputs + branch).astype(jnp.bfloat16)
    back_z, back_x, back_dt, back_out = (
        lax.all_gather(w_z, "dp", axis=0, tiled=True),
        lax.all_gather(w_x, "dp", axis=0, tiled=True),
        lax.all_gather(w_dt, "dp", axis=0, tiled=True),
        lax.all_gather(w_out, "dp", axis=1, tiled=True),
    )
    cot_full = lax.all_gather(cotangent, "tensor", axis=0, tiled=True)
    grad_out_w = jnp.einsum("ti,td->id", mixed, cot_full, preferred_element_type=jnp.float32)
    grad_mixed = jnp.einsum("td,id->ti", cot_full, back_out, preferred_element_type=jnp.float32)
    scaled = grad_mixed * gain_gate
    row_inner = lax.psum(jnp.sum(scaled * gated, axis=-1), "tensor")
    grad_gated = (
        inv_gate[:, None] * scaled - gated * (inv_gate**3 * row_inner / inner_width)[:, None]
    )
    grad_gate_gain = jnp.sum(grad_mixed * gated * inv_gate[:, None], axis=0)
    grad_mixer = grad_gated * gate_act
    grad_z = grad_gated * mixer * silu_slope(z_part)
    grad_z_low = grad_z.astype(jnp.bfloat16)
    grad_w_z = jnp.einsum("td,ti->di", normed, grad_z_low, preferred_element_type=jnp.float32)
    grad_xconv, grad_bcconv, grad_dtraw, grad_dtbias, grad_alog, grad_dskip = mixer_back(grad_mixer)
    grad_xpre_conv = grad_xconv * silu_slope(x_conv_pre)
    seg_padded = jnp.pad(seg_ids, (0, taps_count - 1), constant_values=-1)
    grad_xpre = conv_input_grad(
        jnp.pad(grad_xpre_conv, ((0, taps_count - 1), (0, 0))), kern_x, seg_padded
    )
    grad_kern_x, grad_offset_x = conv_kernel_grad(grad_xpre_conv, x_pre, seg_ids, 0, x_pre.shape[0])
    bc_summed = lax.psum(grad_bcconv, "tensor")
    bc_before = bc_summed * silu_slope(bc_conv_pre)
    padded_rows = jnp.pad(bc_before, ((0, taps_count - 1), (0, 0)))
    extended = lax.dynamic_slice_in_dim(padded_rows, own_start, own_rows + taps_count - 1, 0)
    seg_ext = lax.dynamic_slice_in_dim(seg_padded, own_start, own_rows + taps_count - 1, 0)
    grad_bcpre = conv_input_grad(extended, kern_bcf, seg_ext)
    grad_kern_bc, grad_offset_bc = conv_kernel_grad(
        extended[:own_rows], bc_pre, seg_ids, own_start, own_rows
    )
    grad_x_low = grad_xpre.astype(jnp.bfloat16)
    grad_dt_low = grad_dtraw.astype(jnp.bfloat16)
    grad_bc_low = grad_bcpre.astype(jnp.bfloat16)
    grad_w_x = jnp.einsum("td,ti->di", normed, grad_x_low, preferred_element_type=jnp.float32)
    grad_w_dt = jnp.einsum("td,th->dh", normed, grad_dt_low, preferred_element_type=jnp.float32)
    grad_w_bc = jnp.einsum("td,tn->dn", normed_own, grad_bc_low, preferred_element_type=jnp.float32)
    summed = jnp.einsum("ti,di->td", grad_z_low, back_z, preferred_element_type=jnp.float32)
    summed = summed + jnp.einsum(
        "ti,di->td", grad_x_low, back_x, preferred_element_type=jnp.float32
    )
    grad_normed = lax.psum_scatter(
        summed + jnp.einsum("th,dh->td", grad_dt_low, back_dt, preferred_element_type=jnp.float32),
        "tensor",
        scatter_dimension=0,
        tiled=True,
    )
    grad_normed = grad_normed + jnp.einsum(
        "tn,dn->td", grad_bc_low, full_bc, preferred_element_type=jnp.float32
    )
    scaled_in = grad_normed * gain_in
    grad_gain_in = jnp.sum(grad_normed * unit_rows, axis=0)
    grad_input = inv_rms * (
        scaled_in - unit_rows * jnp.mean(scaled_in * unit_rows, axis=-1, keepdims=True)
    ) + cotangent.astype(jnp.float32)
    red_z, red_x, red_dt, red_out = (
        lax.psum_scatter(grad_w_z, "dp", scatter_dimension=0, tiled=True),
        lax.psum_scatter(grad_w_x, "dp", scatter_dimension=0, tiled=True),
        lax.psum_scatter(grad_w_dt, "dp", scatter_dimension=0, tiled=True),
        lax.psum_scatter(grad_out_w, "dp", scatter_dimension=1, tiled=True),
    )
    red_bc, red_gain, red_kern_bc, red_offset_bc = (
        lax.psum_scatter(grad_w_bc, ("dp", "tensor"), scatter_dimension=0, tiled=True),
        lax.psum_scatter(grad_gain_in, ("dp", "tensor"), scatter_dimension=0, tiled=True),
        lax.psum_scatter(grad_kern_bc, ("dp", "tensor"), scatter_dimension=1, tiled=True),
        lax.psum_scatter(grad_offset_bc, ("dp", "tensor"), scatter_dimension=0, tiled=True),
    )
    red_kern_x, red_offset_x, red_dtbias, red_alog, red_dskip, red_gate = lax.psum(
        (grad_kern_x, grad_offset_x, grad_dtbias, grad_alog, grad_dskip, grad_gate_gain), "dp"
    )
    return (
        out,
        grad_input,
        red_gain,
        red_z,
        red_x,
        red_bc,
        red_dt,
        red_kern_x,
        red_offset_x,
        red_kern_bc,
        red_offset_bc,
        red_dtbias,
        red_alog,
        red_dskip,
        red_gate,
        red_out,
    )


def solution(mesh):
    in_specs = (
        P(("dp", "tensor"), None),
        P(("dp", "tensor"), None),
        P("dp"),
        P(("dp", "tensor")),
        P("dp", "tensor"),
        P("dp", "tensor"),
        P(("dp", "tensor"), None),
        P("dp", "tensor"),
        P(None, "tensor"),
        P("tensor"),
        P(None, ("dp", "tensor")),
        P(("dp", "tensor")),
        P("tensor"),
        P("tensor"),
        P("tensor"),
        P("tensor"),
        P("tensor", "dp"),
    )
    out_specs = (
        P(("dp", "tensor"), None),
        P(("dp", "tensor"), None),
        P(("dp", "tensor")),
        P("dp", "tensor"),
        P("dp", "tensor"),
        P(("dp", "tensor"), None),
        P("dp", "tensor"),
        P(None, "tensor"),
        P("tensor"),
        P(None, ("dp", "tensor")),
        P(("dp", "tensor")),
        P("tensor"),
        P("tensor"),
        P("tensor"),
        P("tensor"),
        P("tensor", "dp"),
    )
    return jax.shard_map(
        per_device, mesh=mesh, in_specs=in_specs, out_specs=out_specs, check_vma=False
    )
```

profile of v0, /device:TPU:0, one launch (start us, length us, event | category | flops | bytes accessed | tf_op | source)
XLA Modules:
  0.0 2377.0 jit_solution(15493860553037997007)
XLA Ops:
  10.4 68.4 %all-reduce.26 = (bf16[1536]{0:T(1024)(128)(2,1)S(1)}, bf16[256]{0:T(256)(128)(2,1)S(1)}) all-reduce(bf16[1536]{0:T(1024)(128)(2,1)S(1)} %dynamic-update-slice, bf16[256]{0:T(256)(128)(2,1)S(1)} %dynamic-update-slice.1), channel_id=1, replica_groups=mesh['dp'=64,'tensor'=2] {'dp','tensor'}, use_global_device_ids=true, to_apply=%add.16 | all-reduce | flops 1792 | bytes 7168
  89.2 310.4 %all-gather = bf16[128,2,4]{2,1,0:T(2,128)(2,1)S(1)} all-gather(bf16[1,2,4]{2,1,0:T(2,128)(2,1)S(1)} %bitcast.275), channel_id=1, replica_groups=mesh['dp'=64,'tensor'=2] {'dp','tensor'}, dimensions={0}, use_global_device_ids=true | all-gather | bytes 2064 | tf_op jit(solution)/shard_map/all_gather | solution.py:143
  401.1 82.4 %all_gather.37 = bf16[1536,24]{1,0:T(8,128)(2,1)} all-gather(bf16[24,24]{1,0:T(8,128)(2,1)S(1)} %copy-done.129), channel_id=1, replica_groups=mesh['dp'=64,'tensor'=2] {'dp'}, dimensions={0}, use_global_device_ids=true | all-gather | bytes 74880 | tf_op jit(solution)/shard_map/all_gather | solution.py:137
  483.6 317.8 %all-gather.1 = bf16[128,12,256]{2,1,0:T(8,128)(2,1)S(1)} all-gather(bf16[1,12,256]{2,1,0:T(8,128)(2,1)S(1)} %bitcast.269), channel_id=1, replica_groups=mesh['dp'=64,'tensor'=2] {'dp','tensor'}, dimensions={0}, use_global_device_ids=true | all-gather | bytes 792576 | tf_op jit(solution)/shard_map/all_gather | solution.py:141
  841.8 15.4 while.34
  866.7 15.9 bitcast_add_fusion.3
  894.8 11.3 multiply_reduce_fusion.11
  914.4 8.7 multiply_reduce_fusion.3
  931.0 9.4 multiply_reduce_fusion.4
  953.8 10.7 fusion.73
  964.5 21.0 fusion.12
  992.2 19.5 while.35
  1013.2 12.9 fusion.74
  1034.0 11.1 bitcast_add_fusion.2
  1063.6 9.8 multiply_reduce_fusion.8
  1098.8 7.4 fusion.128
  1123.7 355.1 %fusion = f32[16,256]{1,0:T(8,128)S(1)} fusion(f32[1536,256]{1,0:T(8,128)} %fusion.143), kind=kCustom, calls=%all-reduce-scatter | all-reduce-scatter fusion | flops 524289 | bytes 1589248
  1495.6 14.5 collective-permute-start.22
  1545.5 275.8 %all-reduce.25 = (f32[4,1536]{1,0:T(4,128)}, f32[1536]{0:T(1024)}, f32[24]{0:T(128)}, f32[24]{0:T(128)}, f32[24]{0:T(128)}, /*index=5*/f32[1536]{0:T(1024)}) all-reduce(f32[4,1536]{1,0:T(4,128)S(1)} %pad_maximum_fusion, f32[1536]{0:T(1024)} %get-tuple-element.379, ...), channel_id=1, replica_groups=mesh['dp'=64,'tensor'=2] {'dp'}, use_global_device_ids=true, to_apply=%region_34.35 | all-reduce | flops 9288 | bytes 74304 | tf_op jit(solution)/shard_map/psum | solution.py:260
  1836.6 19.0 collective-permute-start
  1857.0 21.8 concatenate.8
  1882.7 69.8 %all-reduce.24 = (f32[1536]{0:T(1024)S(1)}, f32[4,256]{1,0:T(4,128)S(1)}, f32[256]{0:T(256)S(1)}) all-reduce(f32[1536]{0:T(1024)S(1)} %get-tuple-element.380, f32[4,256]{1,0:T(4,128)S(1)} %pad_maximum_fusion.1, f32[256]{0:T(256)S(1)} %copy-done.133), channel_id=4, replica_groups=mesh['dp'=64,'tensor'=2] {'dp','tensor'}, use_global_device_ids=true, to_apply=%region_25.26.clone | all-reduce | flops 2816 | bytes 22528
  1958.2 112.0 %reduce-scatter.19.cloned.1.call-done = f32[24,1536]{1,0:T(8,128)} async-done(((f32[1536,1536]{1,0:T(8,128)}), f32[24,1536]{1,0:T(8,128)}) %reduce-scatter.19.cloned.1.call-update) | async-done | bytes 147472 | tf_op jit(solution)/shard_map/reduce_scatter | solution.py:250
  2070.2 299.6 %reduce-scatter.17.cloned.1.call-done = f32[24,1536]{1,0:T(8,128)} async-done(((f32[1536,1536]{1,0:T(8,128)}), f32[24,1536]{1,0:T(8,128)}) %reduce-scatter.17.cloned.1.call-update) | async-done | bytes 147472 | tf_op jit(solution)/shard_map/reduce_scatter | solution.py:249
  (535 shorter events, 294.6 us)
Async XLA Ops:
  7.3 796.2 %all-gather.8.cloned.1.call-start = ((), (), s32[]{:S(2)}) async-start(), calls=%async_computation.6 | async-start | bytes 2359296 | tf_op jit(solution)/shard_map/all_gather | solution.py:151
  81.7 734.1 %all-gather.10.cloned.1.call-start = ((), (), s32[]{:S(2)}) async-start(), calls=%async_computation.7 | async-start | bytes 4792320 | tf_op jit(solution)/shard_map/all_gather | solution.py:136
  82.5 812.3 %all-gather.12.cloned.1.call-start = ((), (), s32[]{:S(2)}) async-start(), calls=%async_computation.8 | async-start | bytes 4792320 | tf_op jit(solution)/shard_map/all_gather | solution.py:135
  83.2 831.2 %all-gather.16.cloned.1.call-start = ((), (), s32[]{:S(2)}) async-start(), calls=%async_computation.11 | async-start | bytes 2359296 | tf_op jit(solution)/shard_map/all_gather | solution.py:195
  83.8 830.7 %all-gather.14.cloned.1.call-start = ((), (), s32[]{:S(2)}) async-start(), calls=%async_computation.9 | async-start | bytes 4792320 | tf_op jit(solution)/shard_map/all_gather | solution.py:138
  84.4 1036.0 %all-reduce.29.cloned.1.call-start = ((), (), s32[]{:S(2)}) async-start(), calls=%async_computation.13 | async-start | bytes 1048576 | tf_op jit(solution)/shard_map/psum | solution.py:215
  1046.0 833.4 %reduce-scatter.15.cloned.1.call-start = ((), (), s32[]{:S(2)}) async-start(), calls=%async_computation.12 | async-start | bytes 4718592 | tf_op jit(solution)/shard_map/reduce_scatter | solution.py:234
  1086.7 867.7 %reduce-scatter.13.cloned.1.call-start = ((), (), s32[]{:S(2)}) async-start(), calls=%async_computation.10 | async-start | bytes 4718592 | tf_op jit(solution)/shard_map/reduce_scatter | solution.py:182
  1095.8 862.4 %reduce-scatter.23.cloned.1.call-start = ((), (), s32[]{:S(2)}) async-start(), calls=%async_computation.17 | async-start | bytes 798720
  1098.7 859.5 %reduce-scatter.21.cloned.1.call-start = ((), (), s32[]{:S(2)}) async-start(), calls=%async_computation.16 | async-start | bytes 9584640 | tf_op jit(solution)/shard_map/reduce_scatter | solution.py:252
  1106.2 963.9 %reduce-scatter.19.cloned.1.call-start = ((), (), s32[]{:S(2)}) async-start(), calls=%async_computation.15 | async-start | bytes 9584640 | tf_op jit(solution)/shard_map/reduce_scatter | solution.py:250
  1112.8 1256.9 %reduce-scatter.17.cloned.1.call-start = ((), (), s32[]{:S(2)}) async-start(), calls=%async_computation.14 | async-start | bytes 9584640 | tf_op jit(solution)/shard_map/reduce_scatter | solution.py:249
  1485.4 24.7 %collective-permute-start.26 = (f32[16,256]{1,0:T(8,128)S(1)}, f32[16,256]{1,0:T(8,128)S(1)}, u32[]{:S(2)}, u32[]{:S(2)}) collective-permute-start(f32[16,256]{1,0:T(8,128)S(1)} %fusion), channel_id=1, source_target_pairs={{0,27},{1,28},{2,29},{3,30},{4,31},{5,32},{6,33},{7,34},{8,35},{9,... | collective-permute-start | bytes 49160
  1486.7 27.8 %collective-permute-start.25 = (f32[16,256]{1,0:T(8,128)S(1)}, f32[16,256]{1,0:T(8,128)S(1)}, u32[]{:S(2)}, u32[]{:S(2)}) collective-permute-start(f32[16,256]{1,0:T(8,128)S(1)} %fusion), channel_id=1, source_target_pairs={{0,26},{1,27},{2,28},{3,29},{4,30},{5,31},{6,32},{7,33},{8,34},{9,... | collective-permute-start | bytes 49160
  1493.0 24.6 %collective-permute-start.24 = (f32[16,256]{1,0:T(8,128)S(1)}, f32[16,256]{1,0:T(8,128)S(1)}, u32[]{:S(2)}, u32[]{:S(2)}) collective-permute-start(f32[16,256]{1,0:T(8,128)S(1)} %fusion), channel_id=1, source_target_pairs={{0,25},{1,26},{2,27},{3,28},{4,29},{5,30},{6,31},{7,32},{8,33},{9,... | collective-permute-start | bytes 49160
  1494.3 24.6 %collective-permute-start.23 = (f32[16,256]{1,0:T(8,128)S(1)}, f32[16,256]{1,0:T(8,128)S(1)}, u32[]{:S(2)}, u32[]{:S(2)}) collective-permute-start(f32[16,256]{1,0:T(8,128)S(1)} %fusion), channel_id=1, source_target_pairs={{0,24},{1,25},{2,26},{3,27},{4,28},{5,29},{6,30},{7,31},{8,32},{9,... | collective-permute-start | bytes 49160
  1495.6 25.6 %collective-permute-start.22 = (f32[16,256]{1,0:T(8,128)S(1)}, f32[16,256]{1,0:T(8,128)S(1)}, u32[]{:S(2)}, u32[]{:S(2)}) collective-permute-start(f32[16,256]{1,0:T(8,128)S(1)} %fusion), channel_id=1, source_target_pairs={{0,23},{1,24},{2,25},{3,26},{4,27},{5,28},{6,29},{7,30},{8,31},{9,... | collective-permute-start | bytes 49160
  1531.3 290.0 %collective-permute-start.14 = (f32[16,256]{1,0:T(8,128)S(1)}, f32[16,256]{1,0:T(8,128)S(1)}, u32[]{:S(2)}, u32[]{:S(2)}) collective-permute-start(f32[16,256]{1,0:T(8,128)S(1)} %fusion), channel_id=1, source_target_pairs={{0,15},{1,16},{2,17},{3,18},{4,19},{5,20},{6,21},{7,22},{8,23},{9,... | collective-permute-start | bytes 49160
  1532.7 290.0 %collective-permute-start.13 = (f32[16,256]{1,0:T(8,128)S(1)}, f32[16,256]{1,0:T(8,128)S(1)}, u32[]{:S(2)}, u32[]{:S(2)}) collective-permute-start(f32[16,256]{1,0:T(8,128)S(1)} %fusion), channel_id=1, source_target_pairs={{0,14},{1,15},{2,16},{3,17},{4,18},{5,19},{6,20},{7,21},{8,22},{9,... | collective-permute-start | bytes 49160
  1534.7 289.3 %collective-permute-start.12 = (f32[16,256]{1,0:T(8,128)S(1)}, f32[16,256]{1,0:T(8,128)S(1)}, u32[]{:S(2)}, u32[]{:S(2)}) collective-permute-start(f32[16,256]{1,0:T(8,128)S(1)} %fusion), channel_id=1, source_target_pairs={{0,13},{1,14},{2,15},{3,16},{4,17},{5,18},{6,19},{7,20},{8,21},{9,... | collective-permute-start | bytes 49160
  1539.9 285.4 %collective-permute-start.11 = (f32[16,256]{1,0:T(8,128)S(1)}, f32[16,256]{1,0:T(8,128)S(1)}, u32[]{:S(2)}, u32[]{:S(2)}) collective-permute-start(f32[16,256]{1,0:T(8,128)S(1)} %fusion), channel_id=1, source_target_pairs={{0,12},{1,13},{2,14},{3,15},{4,16},{5,17},{6,18},{7,19},{8,20},{9,... | collective-permute-start | bytes 49160
  1541.5 285.1 %collective-permute-start.10 = (f32[16,256]{1,0:T(8,128)S(1)}, f32[16,256]{1,0:T(8,128)S(1)}, u32[]{:S(2)}, u32[]{:S(2)}) collective-permute-start(f32[16,256]{1,0:T(8,128)S(1)} %fusion), channel_id=1, source_target_pairs={{0,11},{1,12},{2,13},{3,14},{4,15},{5,16},{6,17},{7,18},{8,19},{9,... | collective-permute-start | bytes 49160
  1830.1 25.6 %collective-permute-start.4 = (f32[16,256]{1,0:T(8,128)S(1)}, f32[16,256]{1,0:T(8,128)S(1)}, u32[]{:S(2)}, u32[]{:S(2)}) collective-permute-start(f32[16,256]{1,0:T(8,128)S(1)} %fusion), channel_id=1, source_target_pairs={{0,5},{1,6},{2,7},{3,8},{4,9},{5,10},{6,11},{7,12},{8,13},{9,14},{... | collective-permute-start | bytes 49160
  1831.5 24.1 %collective-permute-start.3 = (f32[16,256]{1,0:T(8,128)S(1)}, f32[16,256]{1,0:T(8,128)S(1)}, u32[]{:S(2)}, u32[]{:S(2)}) collective-permute-start(f32[16,256]{1,0:T(8,128)S(1)} %fusion), channel_id=1, source_target_pairs={{0,4},{1,5},{2,6},{3,7},{4,8},{5,9},{6,10},{7,11},{8,12},{9,13},{1... | collective-permute-start | bytes 49160
  (166 other events, 10640.6 us)
Sparse Core Ops, SparseCore 0:
  81.8 27.6 all-gather.7
  111.3 106.0 all-gather.9
  219.1 106.0 all-gather.11
  326.6 30.5 all-gather.15
  358.8 106.4 all-gather.13
  1046.2 31.6 all-reduce.28
  1086.8 42.4 reduce-scatter.14
  1131.6 48.8 reduce-scatter.12
  1183.5 285.8 reduce-scatter.22
  1472.2 296.9 reduce-scatter.20
  1772.2 297.9 reduce-scatter.18
  2073.0 296.6 reduce-scatter.16
where the time goes:
time: 2390 us; the launch traced here: 2380 us
  blocking collectives  1490 us (62%)
  waiting for transfers between devices  416 us (17%)
  matrix products  165 us (7%)
  local copies, waits for them, and re-layouts  123 us (5%)
  starting transfers between devices  91.9 us (4%)
  other arithmetic  70.1 us (3%)
    unnamed x3, blocking collectives  493 us
    all_gather x1, blocking collectives, per_device(): lax.all_gather(w_bc, ('dp', 'tensor'), axis=0, tiled=True)  318 us
    all_gather x1, blocking collectives, per_device(): lax.all_gather(conv_bc_w, ('dp', 'tensor'), axis=1, tiled=True)  310 us
    reduce_scatter x1, waiting for transfers between devices, per_device(): lax.psum_scatter(grad_w_z, 'dp', scatter_dimension=0, tiled=True)  300 us
    psum x1, blocking collectives, per_device(): lax.psum((grad_kern_x, grad_offset_x, grad_dtbias, grad_alog, grad_dskip,...  276 us
    reduce_scatter x1, waiting for transfers between devices, per_device(): lax.psum_scatter(grad_w_x, 'dp', scatter_dimension=0, tiled=True)  112 us
    unnamed x33, starting transfers between devices  91.4 us
    all_gather x1, blocking collectives, per_device(): lax.all_gather(w_dt, 'dp', axis=0, tiled=True)  82.4 us
  transfers between devices with their start and end apart: 44, of which 3 were waited for; matrix products, arithmetic and copies ran while one was open for 24% of the time, Pallas kernels for 0%

commit v1 on v0

v1 whole, which is shorter than its diff:
```python
import functools
import jax
import jax.numpy as jnp
from jax import lax
from jax.experimental import pallas as pl
from jax.experimental.pallas import tpu as pltpu
from jax.sharding import PartitionSpec as P

CONV = 4
SCAN_BLOCK = 256
EPS = 1e-05
MESH = pl.DeviceIdType.MESH
BF = jnp.bfloat16
F32 = jnp.float32

D = 1536
SEQ = 512
HALF = 768
WIDTHS = (256, 768, 768, 768)
STARTS = (0, 128, 512, 896)
PACKED = 1280


class Place:
    def __init__(self):
        dp = lax.axis_index("dp")
        tz = lax.axis_index("tensor")
        self.dp, self.tz = dp, tz
        self.core = dp % 2
        self.zlo = (dp // 2) % 2
        self.x = (dp // 4) % 4
        self.y = dp // 16
        c = self.core
        self.f = self.x * (1 - c) + self.y * c
        self.s = self.y * (1 - c) + self.x * c
        self.quad = dp % 4
        self.partner = (dp - c + (1 - c), tz)
        self.zmate = (dp - 2 * self.zlo + 2 * (1 - self.zlo), tz)

    def at(self, y, x, zlo, core, tz):
        return (((y * 4 + x) * 2 + zlo) * 2 + core, tz)

    def xy(self, dy, dx):
        return self.at((self.y + dy + 4) % 4, (self.x + dx + 4) % 4, self.zlo, self.core, self.tz)

    def first(self, d):
        c = self.core
        return self.xy(d * c, d * (1 - c))

    def second(self, d):
        c = self.core
        return self.xy(d * (1 - c), d * c)

    def member(self, r):
        return (self.dp - self.quad + (self.quad + r) % 4, self.tz)

    def ring(self, d):
        z = (self.tz * 2 + self.zlo + d + 4) % 4
        return self.at(self.y, self.x, z % 2, self.core, z // 2)

    def ring_half(self, d):
        return ((self.tz * 2 + self.zlo + d + 4) % 4) // 2

    def block(self, f, s):
        c = self.core
        return s * (1 - c) + f * c, f * (1 - c) + s * c

    def greet(self, more=False):
        barrier = pltpu.get_barrier_semaphore()
        others = [self.member(1), self.member(2), self.member(3)]
        others += [self.xy(0, 1), self.xy(0, -1), self.xy(1, 0), self.xy(-1, 0)]
        others += [self.ring(1), self.ring(-1)]
        if more:
            others += [self.xy(0, 2), self.xy(2, 0)]
        others += [self.ring(2)]
        for other in others:
            pl.semaphore_signal(barrier, inc=1, device_id=other, device_id_type=MESH)
        pl.semaphore_wait(barrier, len(others))


def send(src, dst, ssem, rsem, device):
    copy = pltpu.make_async_remote_copy(
        src_ref=src, dst_ref=dst, send_sem=ssem, recv_sem=rsem, device_id=device, device_id_type=MESH
    )
    copy.start()
    return copy


def wait_bytes(ref, sem):
    pltpu.make_async_copy(ref, ref, sem).wait()


class Gather:
    COUNT = 15

    def __init__(self, place, shard, stage, full, ssem, rsem, index):
        self.p, self.shard, self.stage, self.full = place, shard, stage, full
        self.ss = lambda k: ssem.at[index, k]
        self.rs = lambda k: rsem.at[index, k]
        self.lo = STARTS[index]
        self.width = WIDTHS[index]
        self.half = self.width // 2
        self.sent = []

    def cols(self):
        return pl.ds(self.lo, self.half)

    def start(self):
        p = self.p
        for r in (1, 2, 3):
            other_core = (p.quad + r) % 2
            self.sent.append(
                send(
                    self.shard.at[other_core, :, self.cols()],
                    self.stage.at[p.quad, :, self.cols()],
                    self.ss(r - 1),
                    self.rs(r - 1),
                    p.member(r),
                )
            )

    def first(self):
        p = self.p
        for copy in self.sent[:3]:
            copy.wait_recv()
        own = self.shard[p.core, :, self.lo : self.lo + self.half]
        rows = []
        for j in range(4):
            piece = jnp.where(p.quad == j, own, self.stage[j, :, self.lo : self.lo + self.half])
            piece = piece.astype(F32)
            rows.append(jnp.concatenate([piece[:24], piece[24:]], axis=1))
        self.full[p.core, p.y, p.x] = jnp.concatenate(rows, axis=0).astype(BF)
        block = self.full.at[p.core, p.y, p.x]
        self.sent.append(send(block, block, self.ss(3), self.rs(3), p.first(1)))
        self.sent.append(send(block, block, self.ss(4), self.rs(4), p.first(-1)))

    def first_far(self):
        p = self.p
        a, b = self.sent[3:5]
        a.wait_recv()
        yy, xx = p.block((p.f + 3) % 4, p.s)
        part = self.full.at[p.core, yy, xx, pl.ds(0, 48)]
        self.sent.append(send(part, part, self.ss(5), self.rs(5), p.first(1)))
        b.wait_recv()
        yy, xx = p.block((p.f + 1) % 4, p.s)
        part = self.full.at[p.core, yy, xx, pl.ds(48, 48)]
        self.sent.append(send(part, part, self.ss(6), self.rs(6), p.first(-1)))

    def _blocks(self, s, ks, k_sem, device):
        p = self.p
        for k in ks:
            yy, xx = p.block(k, s)
            part = self.full.at[p.core, yy, xx]
            send(part, part, self.ss(k_sem), self.rs(k_sem), device)

    def second(self):
        p = self.p
        for copy in self.sent[5:7]:
            copy.wait_recv()
        self._blocks(p.s, range(4), 7, p.second(1))
        self._blocks(p.s, range(4), 8, p.second(-1))
        self._blocks(p.s, range(4), 11, p.partner)

    def second_far(self):
        p = self.p
        wait_bytes(self.full.at[0, 0], self.rs(7))
        self._blocks((p.s + 3) % 4, (0, 1), 9, p.second(1))
        wait_bytes(self.full.at[0, 0], self.rs(8))
        self._blocks((p.s + 1) % 4, (2, 3), 10, p.second(-1))
        self._blocks((p.s + 3) % 4, range(4), 12, p.partner)
        self._blocks((p.s + 1) % 4, range(4), 13, p.partner)

    def last(self):
        p = self.p
        wait_bytes(self.full.at[0, 0, pl.ds(0, 2)], self.rs(9))
        wait_bytes(self.full.at[0, 0, pl.ds(0, 2)], self.rs(10))
        self._blocks((p.s + 2) % 4, range(4), 14, p.partner)

    def ready(self):
        for k in (11, 12, 13, 14):
            wait_bytes(self.full.at[0, 0], self.rs(k))

    def finish(self):
        for copy in self.sent:
            copy.wait_send()
        for k in (7, 8, 11, 12, 13, 14):
            wait_bytes(self.full.at[0, 0], self.ss(k))
        for k in (9, 10):
            wait_bytes(self.full.at[0, 0, pl.ds(0, 2)], self.ss(k))


class Cross:
    def __init__(self, place, relay, ssem, rsem, index):
        self.p, self.relay = place, relay
        self.ss = lambda k: ssem.at[index, k]
        self.rs = lambda k: rsem.at[index, k]

    def start(self, up, down):
        send(up, self.relay.at[0], self.ss(0), self.rs(0), self.p.ring(1))
        send(down, self.relay.at[1], self.ss(1), self.rs(1), self.p.ring(-1))

    def forward(self, up, down):
        p = self.p
        wait_bytes(self.relay.at[0], self.rs(0))
        send(self.relay.at[0], up(p.ring_half(-1)), self.ss(2), self.rs(2), p.ring(1))
        wait_bytes(self.relay.at[1], self.rs(1))
        send(self.relay.at[1], down(p.ring_half(1)), self.ss(3), self.rs(3), p.ring(-1))

    def ready(self):
        wait_bytes(self.relay.at[0], self.rs(2))
        wait_bytes(self.relay.at[1], self.rs(3))

    def release(self):
        wait_bytes(self.relay.at[0], self.ss(0))
        wait_bytes(self.relay.at[1], self.ss(1))

    def finish(self):
        wait_bytes(self.relay.at[0], self.ss(2))
        wait_bytes(self.relay.at[1], self.ss(3))


CHUNK = 256
HEADS = 4
TILE = 64
LOG2E = 1.4426950408889634
HIGH = lax.Precision.HIGHEST
NEVER = -1e30


def split(v):
    hi = v.astype(BF)
    return hi, (v - hi.astype(F32)).astype(BF)


def dot(a, b):
    return jnp.dot(a, b, preferred_element_type=F32)


def dot_nt(a, b):
    return lax.dot_general(a, b, (((1,), (1,)), ((), ())), preferred_element_type=F32)


def dot_tn(a, b):
    return lax.dot_general(a, b, (((0,), (0,)), ((), ())), preferred_element_type=F32)


def sig(v):
    return 0.5 * jnp.tanh(0.5 * v) + 0.5


def side(*parts):
    return jnp.concatenate(parts, axis=1)


def below(*parts):
    return jnp.concatenate(parts, axis=0)


def fine(product, a, b):
    a_hi, a_lo = split(a)
    b_hi, b_lo = split(b)
    if product is dot:
        return dot(side(a_hi, a_hi, a_lo), below(b_hi, b_lo, b_hi))
    if product is dot_nt:
        return dot_nt(side(a_hi, a_hi, a_lo), side(b_hi, b_lo, b_hi))
    return product(a_hi, b_hi) + (product(a_hi, b_lo) + product(a_lo, b_hi))


def lanes_in(width, low, high):
    lane = lax.broadcasted_iota(jnp.int32, (1, width), 1)
    return ((lane >= low) & (lane < high)).astype(F32)


def head_columns(table, c):
    turned = pltpu.roll(table, (128 - HEADS * c) % 128, 1)
    return [jnp.broadcast_to(turned[:, k : k + 1], table.shape) for k in range(HEADS)]


def on_channels(columns):
    lane = lax.broadcasted_iota(jnp.int32, columns[0].shape, 1)
    return side(jnp.where(lane < 64, columns[0], columns[1]), jnp.where(lane < 64, columns[2], columns[3]))


def head_of_channel(c):
    lane = lax.broadcasted_iota(jnp.int32, (CHUNK, 128), 0)
    head = lax.broadcasted_iota(jnp.int32, (CHUNK, 128), 1)
    return head - (HEADS * c + lane // 64)


def conv_pre(values, taps, same):
    summed = taps[4:5, :] + taps[3:4, :] * values
    for d in (1, 2, 3):
        summed = summed + taps[3 - d : 4 - d, :] * (pltpu.roll(values, d, 0) * same[:, d : d + 1])
    return summed


def slope_of(values, sigma):
    return sigma * (1.0 + values * (1.0 - sigma))


def doc_bias(b, segc, segr, flip):
    rows = segc[256 * b : 256 * b + 256, 0:1]
    cols = segr[0:1, 256 * b : 256 * b + 256]
    i = lax.broadcasted_iota(jnp.int32, (256, 256), 0)
    j = lax.broadcasted_iota(jnp.int32, (256, 256), 1)
    order = (j >= i) if flip else (i >= j)
    return jnp.where(order & (rows == cols), 0.0, NEVER)


def twice(column, width):
    return column if width == 128 else side(column, column)


def apart(values):
    return [values * lanes_in(CHUNK, 64 * k, 64 * k + 64).astype(BF) for k in range(HEADS)]


def packed(values, k, swapped, first, second):
    tile = slice(128 * (k // 2), 128 * (k // 2) + 128)
    left = lanes_in(128, 0, 64).astype(BF)
    right = lanes_in(128, 64, 128).astype(BF)
    here, there = (values, swapped) if k % 2 == 0 else (swapped, values)
    low = here[first][:, tile] * left
    return low if second is None else low + there[second][:, tile] * right


def swap(values):
    return side(pltpu.roll(values[:, 0:128], 64, 1), pltpu.roll(values[:, 128:256], 64, 1))


def tile(full, h, lo, width):
    value = full[h, :, :, :, pl.ds(lo, width)]
    return value.reshape(D, width)


def columns_of(c):
    return pl.ds(pl.multiple_of(c * CHUNK, CHUNK), CHUNK)


def front_kernel(
    wx_in, wz_in, wo_in, tiny, segr, chan_in, xin, cin,
    o_normed_t, o_cot_t, o_pre, o_z, o_gm, o_small, o_aux, o_ws, o_wx, o_wz, o_wo,
    o_xcp, o_y_low, o_sums, o_bcc, o_bc, o_cum, o_cum_t, o_step, o_same, o_segc, o_taps, o_chans, o_heads, o_mixed, o_normed_far, o_cot_far,
    shard, tiny_got, stage, w_s, w_x, w_z, w_o, x_all, c_all, relay_x, relay_c,
    normed, normed_t, cot_t, pre, zed, gm, small, aux,
    xcp, y, y_low, sums, bcc, bc, cum, cum_t, step, same, segc, taps, chans, heads,
    bias, affinity, b_t, sums_t, sums_got, pre_low, normed_far, cot_far,
    g_ssem, g_rsem, c_ssem, c_rsem, t_ssem, t_rsem, l_sem,
):
    p = Place()
    p.greet()
    gathers = [Gather(p, shard, stage, full, g_ssem, g_rsem, i) for i, full in enumerate((w_s, w_x, w_z, w_o))]
    gs, gx, gz, go = gathers
    cross_x = Cross(p, relay_x, c_ssem, c_rsem, 0)
    cross_c = Cross(p, relay_c, c_ssem, c_rsem, 1)
    local = []
    count = iter(range(32))

    def store(*pairs):
        for src, dst in pairs:
            copy = pltpu.make_async_copy(src, dst, l_sem.at[next(count)])
            copy.start()
            local.append(copy)

    def fold_in(value, lo):
        for h in range(2):
            left = value[:, HALF * h : HALF * h + 384]
            right = value[:, HALF * h + 384 : HALF * h + HALF]
            shard[h, :, lo : lo + 384] = jnp.concatenate([left, right], axis=0).astype(BF)

    tiny_copy = send(tiny.at[:, pl.ds(0, 384)], tiny_got, t_ssem.at[0], t_rsem.at[0], p.ring(2))
    fold_in(wx_in[...].astype(F32), STARTS[1])
    gx.start()
    cross_x.start(xin.at[pl.ds(0, 128)], xin.at[pl.ds(128, 128)])
    fold_in(wz_in[...].astype(F32), STARTS[2])
    gz.start()
    fold_in(wo_in[...].astype(F32), STARTS[3])
    go.start()
    tiny_copy.wait_recv()
    both = tiny[:, 0:384] + tiny_got[...]
    shard[0, :, 0:128] = jnp.concatenate([both[:, 0:128], tiny[:, 384:512]], axis=0).astype(BF)
    shard[1, :, 0:128] = jnp.concatenate([both[:, 128:256], both[:, 256:384]], axis=0).astype(BF)
    gs.start()
    cross_c.start(cin.at[pl.ds(0, 128)], cin.at[pl.ds(128, 128)])
    gx.first()
    gs.first()
    gx.first_far()
    gs.first_far()
    gx.second()
    gs.second()
    gz.first()
    go.first()
    x_all[p.tz] = xin[...]
    c_all[p.tz] = cin[...]

    ids = jnp.broadcast_to(segr[0:1, :], (128, SEQ)).T
    segc[...] = ids
    place = lax.broadcasted_iota(jnp.int32, (SEQ, 128), 0)
    lane = lax.broadcasted_iota(jnp.int32, (SEQ, 128), 1)
    table = jnp.where(lane == 4, (ids == ids[255:256]).astype(F32), jnp.where(lane == 0, 1.0, 0.0))
    for d in (1, 2, 3):
        close = (pltpu.roll(ids, d, 0) == ids) & (place >= d)
        table = jnp.where(lane == d, close.astype(F32), table)
    same[...] = table
    heads[...] = jnp.zeros_like(heads)
    heads[0:1, :] = chan_in[6:7, 0:128]
    heads[1:2, :] = jnp.where(lane[0:1] < 24, -jnp.exp(chan_in[6:7, 128:256]), 0.0)
    chans[...] = chan_in[...]
    skips = jnp.broadcast_to(chan_in[6:7, 256:384], (8, 128))
    for c in range(D // CHUNK):
        chans[6:7, CHUNK * c : CHUNK * c + CHUNK] = on_channels(head_columns(skips, c))[0:1]

    gs.second_far()
    gz.first_far()
    go.first_far()
    cross_x.forward(lambda t: x_all.at[t, pl.ds(0, 128)], lambda t: x_all.at[t, pl.ds(128, 128)])
    gs.last()
    gx.second_far()
    gz.second()
    gs.ready()
    column = w_s[1, :, :, :, 128:256].reshape(D, 128).astype(F32)
    aux[...] = column.T[:8]
    row = lax.broadcasted_iota(jnp.int32, (D, 256), 0)
    wide = lax.broadcasted_iota(jnp.int32, (D, 256), 1)
    pick = (row == 12 * (wide // 2) + wide % 2).astype(F32).astype(BF)
    found = dot(aux[...].astype(BF), pick)
    taps[...] = jnp.concatenate([found[1:6], jnp.zeros((3, 256), F32)], axis=0)
    cross_x.ready()
    gain = aux[0:1, :]

    @pl.loop(0, 32)
    def _(i):
        rows = x_all[i // 16, pl.ds(pl.multiple_of((i % 16) * 16, 16), 16), :].astype(F32)
        inv = lax.rsqrt(jnp.mean(rows * rows, axis=-1, keepdims=True) + EPS)
        normed[pl.ds(pl.multiple_of(i * 16, 16), 16), :] = (rows * inv * gain).astype(BF)

    gx.last()
    go.second()
    for h in range(2):
        small[:, 256 * h : 256 * h + 256] = dot(normed[...], tile(w_s, h, 0, 256))

    value = jnp.concatenate([small[:, 0:128], small[:, 256:384]], axis=1)
    value = conv_pre(value, taps, same)
    bcc[...] = value
    bc[...] = value * sig(value)
    raw = small[:, 128:256] + heads[0:1, :]
    soft = jnp.maximum(raw, 0.0) + jnp.log1p(jnp.exp(-jnp.abs(raw)))
    step[...] = soft
    decay = soft * heads[1:2, :]
    i = lax.broadcasted_iota(jnp.int32, (256, 256), 0)
    j = lax.broadcasted_iota(jnp.int32, (256, 256), 1)
    lower = (i >= j).astype(F32)
    for b in range(2):
        rows = slice(256 * b, 256 * b + 256)
        cum[rows, :] = LOG2E * jnp.dot(lower, decay[rows], precision=HIGH, preferred_element_type=F32)
        bias[b] = doc_bias(b, segc, segr, False)
        affinity[b] = fine(dot_nt, bc[rows, 128:256], bc[rows, 0:128])
    cum_turned = cum[...].T
    for h in range(24):
        cum_t[h] = cum_turned[h : h + 1]
    b_t[...] = bc[0:256, 0:128].T

    normed_t[...] = normed[...].astype(F32).T.astype(BF)
    store((normed_t, o_normed_t))
    give_normed = send(normed_t, normed_far, t_ssem.at[2], t_rsem.at[2], p.partner)
    gx.ready()

    def project(lhs, full, out):
        for h in range(2):
            @pl.loop(0, 3)
            def _(t):
                lo = pl.multiple_of(t * 256, 256)
                out[:, pl.ds(pl.multiple_of(h * HALF + t * 256, 256), 256)] = dot(lhs[...], tile(full, h, lo, 256))

    project(normed, w_x, pre)
    gz.second_far()
    cross_c.forward(lambda t: c_all.at[t, pl.ds(0, 128)], lambda t: c_all.at[t, pl.ds(128, 128)])
    store((w_s, o_ws), (w_x, o_wx), (small, o_small), (aux, o_aux), (bcc, o_bcc), (bc, o_bc), (cum, o_cum),
          (cum_t, o_cum_t), (step, o_step), (same, o_same), (segc, o_segc), (taps, o_taps), (chans, o_chans), (heads, o_heads))

    def scan_chunk(c):
        cols = columns_of(c)
        pre_low[:, cols] = pre[:, cols].astype(BF)
        value = conv_pre(pre[:, cols], chans[:, cols], same)
        xcp[:, cols] = value
        xc = value * sig(value)
        columns = head_columns(cum[...], c)
        cums = on_channels(columns)
        scaled = on_channels(head_columns(step[...], c)) * xc
        low, low_rest = split(scaled)
        x_hi, x_lo = apart(low), apart(low_rest)
        linked = same[:, 4:5]
        tail = jnp.exp2(cums[255:256] - cums[0:256]) * linked[0:256]
        state = fine(dot, b_t[...], tail * scaled[0:256])
        across = jnp.exp2(cums[256:512]) * linked[256:512] * fine(dot, bc[256:512, 128:256], state)
        for b in range(2):
            rows = slice(256 * b, 256 * b + 256)
            parts = []
            for k in range(HEADS):
                gap = twice(columns[k][rows], 256) - cum_t[HEADS * c + k, :, rows]
                parts.append(split(jnp.exp2(gap + bias[b]) * affinity[b]))
            m_hi = side(*[part[0] for part in parts])
            m_lo = side(*[part[1] for part in parts])
            both = dot(below(m_hi, m_lo), below(*[v[rows] for v in x_hi]))
            rest = both[256:512] + dot(m_hi, below(*[v[rows] for v in x_lo]))
            total = both[0:256]
            if b:
                total = total + across
            y_low[rows, cols] = total
            y[rows, cols] = total + rest

    pl.loop(0, 2)(scan_chunk)
    gz.last()
    go.second_far()
    pl.loop(2, 4)(scan_chunk)
    go.last()
    pl.loop(4, 6)(scan_chunk)
    store((xcp, o_xcp), (y_low, o_y_low), (pre_low, o_pre))
    pre_stored = local[-1]
    gz.ready()
    store((w_z, o_wz))
    project(normed, w_z, zed)
    store((zed, o_z))
    cross_c.ready()
    cot_t[...] = c_all[...].reshape(SEQ, D).astype(F32).T.astype(BF)
    store((cot_t, o_cot_t))
    give_cot = send(cot_t, cot_far, t_ssem.at[3], t_rsem.at[3], p.partner)
    go.ready()
    store((w_o, o_wo))
    project(c_all.reshape(SEQ, D), w_o, gm)
    store((gm, o_gm))

    @pl.loop(0, SEQ // 32)
    def _(i):
        rows = pl.ds(pl.multiple_of(i * 32, 32), 32)
        squares = jnp.zeros((32, CHUNK), F32)
        inner = jnp.zeros((32, CHUNK), F32)
        for c in range(D // CHUNK):
            cols = slice(CHUNK * c, CHUNK * c + CHUNK)
            value = xcp[rows, cols]
            gate = zed[rows, cols]
            total = y[rows, cols] + chans[6:7, cols] * (value * sig(value))
            gated = total * (gate * sig(gate))
            pre[rows, cols] = gated
            squares += gated * gated
            inner += gm[rows, cols] * chans[5:6, cols] * gated
        spot = lax.broadcasted_iota(jnp.int32, (32, 128), 1)
        first = jnp.sum(squares, axis=1, keepdims=True)
        second = jnp.sum(inner, axis=1, keepdims=True)
        sums[rows, :] = jnp.where(spot == 0, first, jnp.where(spot == 1, second, 0.0))

    give_normed.wait_recv()
    store((normed_far, o_normed_far))
    both_sums = sums[...]
    sums_t[...] = both_sums.T[:8]
    sums_copy = send(sums_t, sums_got, t_ssem.at[1], t_rsem.at[1], p.ring(2))
    for gather in gathers:
        gather.finish()
    for cross in (cross_x, cross_c):
        cross.release()
        cross.finish()
    sums_copy.wait_recv()
    total = jnp.concatenate([sums_t[...] + sums_got[...], jnp.zeros((120, SEQ), F32)], axis=0)
    sums[...] = total.T
    store((sums, o_sums))

    pre_stored.wait()
    local[:] = [copy for copy in local if copy is not pre_stored]

    @pl.loop(0, SEQ // 16)
    def _(i):
        rows = pl.ds(pl.multiple_of(i * 16, 16), 16)
        inv = lax.rsqrt(sums[rows, 0:1] * (1.0 / 3072) + EPS)
        pre_low[rows, :] = (pre[rows, :] * inv * chans[5:6, :]).astype(BF)

    store((pre_low, o_mixed))
    give_cot.wait_recv()
    store((cot_far, o_cot_far))
    give_normed.wait_send()
    give_cot.wait_send()
    tiny_copy.wait_send()
    sums_copy.wait_send()
    for copy in local:
        copy.wait()


def front(args):
    any_space = pl.BlockSpec(memory_space=pl.ANY)
    vmem = pl.BlockSpec(memory_space=pltpu.VMEM)
    wide = lambda w: ((2, 4, 4, 96, w), BF)
    full = ((SEQ, D), F32)
    rows = ((SEQ, 128), F32)
    turned = ((D, SEQ), BF)
    eight = ((8, D), F32)
    out_types = [
        turned, turned, ((SEQ, D), BF), full, full, ((SEQ, 512), F32), eight, wide(256), wide(HALF), wide(HALF), wide(HALF),
        full, full, rows, ((SEQ, 256), F32), ((SEQ, 256), F32), rows, ((24, 1, SEQ), F32), rows, rows, rows,
        ((8, 256), F32), eight, ((8, 128), F32), ((SEQ, D), BF), turned, turned,
    ]
    halves = ((2, 256, D), BF)
    relay = ((2, 128, D), BF)
    square = ((2, 256, 256), F32)
    scratch_types = [
        ((2, 48, PACKED), BF), ((24, 384), F32), ((4, 48, PACKED), BF), wide(256), wide(HALF), wide(HALF), wide(HALF),
        halves, halves, relay, relay,
        ((SEQ, D), BF), turned, turned, full, full, full, ((SEQ, 512), F32), eight,
        full, full, full, rows, ((SEQ, 256), F32), ((SEQ, 256), F32), rows, ((24, 1, SEQ), F32), rows, rows, rows,
        ((8, 256), F32), eight, ((8, 128), F32),
        square, square, ((128, 256), F32), ((8, SEQ), F32), ((8, SEQ), F32),
        ((SEQ, D), BF), turned, turned,
    ]
    sems = [(4, Gather.COUNT), (4, Gather.COUNT), (2, 4), (2, 4), (4,), (4,), (32,)]
    return pl.pallas_call(
        front_kernel,
        out_shape=[jax.ShapeDtypeStruct(*t) for t in out_types],
        in_specs=[vmem] * len(args),
        out_specs=[any_space] * len(out_types),
        scratch_shapes=[pltpu.VMEM(*t) for t in scratch_types] + [pltpu.SemaphoreType.DMA(s) for s in sems],
        compiler_params=pltpu.CompilerParams(
            collective_id=0, has_side_effects=True, vmem_limit_bytes=62 * 1024 * 1024
        ),
        cost_estimate=pl.CostEstimate(flops=2 * SEQ * D * 6000, bytes_accessed=60_000_000, transcendentals=8_000_000),
    )(*args)


class Scatter:
    COUNT = 11

    def __init__(self, place, lhs_t, lhs_far, rhs, rhs_far, width, own, bufs, result, ssem, rsem, index):
        self.p, self.lhs_t, self.lhs_far, self.rhs, self.rhs_far, self.width = place, lhs_t, lhs_far, rhs, rhs_far, width
        self.own, self.result = own, result
        self.rb1, self.rb2, self.ra1, self.ra2, self.zs, self.zr, self.keep, self.ds = bufs
        self.ss = lambda k: ssem.at[index, k]
        self.rs = lambda k: rsem.at[index, k]

    def give(self):
        p = self.p
        send(self.rhs(1 - p.core), self.rhs_far, self.ss(0), self.rs(0), p.partner)

    def own_half(self):
        p = self.p
        wait_bytes(self.rhs_far, self.rs(0))
        mine = self.rhs(p.core)

        @pl.loop(0, 2)
        def _(i):
            rows = pl.ds(pl.multiple_of(i * HALF, 128), HALF)
            both = side(self.lhs_t[rows, :], self.lhs_far[rows, :])
            places = pl.ds(2 * i, 2)
            for lo in range(0, self.width, 256):
                cols = slice(lo, lo + 256)
                value = dot(both, below(mine[:, cols], self.rhs_far[:, cols]))
                self.own[places, :, :, cols] = value.reshape(2, 4, 96, 256).astype(BF)

        far = (p.s + 2) % 4
        self._group(far, (0, 1), self.rb1.at[0], 1, p.second(1))
        self._group(far, (2, 3), self.rb1.at[1], 2, p.second(-1))

    def _group(self, s, ks, dst, k_sem, device):
        p = self.p
        for i, k in enumerate(ks):
            yy, xx = p.block(k, s)
            send(self.own.at[yy, xx], dst.at[i], self.ss(k_sem), self.rs(k_sem), device)

    def _add(self, f, s, terms):
        yy, xx = self.p.block(f, s)
        value = self.own[yy, xx].astype(F32)
        for term in terms:
            value = value + term.astype(F32)
        self.own[yy, xx] = value.astype(BF)

    def second(self):
        p = self.p
        wait_bytes(self.rb1.at[0], self.rs(1))
        for i, k in enumerate((0, 1)):
            self._add(k, (p.s + 1) % 4, [self.rb1[0, i]])
        self._group((p.s + 1) % 4, range(4), self.rb2.at[0], 3, p.second(1))
        wait_bytes(self.rb1.at[1], self.rs(2))
        for i, k in enumerate((2, 3)):
            self._add(k, (p.s + 3) % 4, [self.rb1[1, i]])
        self._group((p.s + 3) % 4, range(4), self.rb2.at[1], 4, p.second(-1))

    def first_far(self):
        p = self.p
        wait_bytes(self.rb2.at[0], self.rs(3))
        wait_bytes(self.rb2.at[1], self.rs(4))
        for k in range(4):
            self._add(k, p.s, [self.rb2[0, k], self.rb2[1, k]])
        yy, xx = p.block((p.f + 2) % 4, p.s)
        send(self.own.at[yy, xx, pl.ds(0, 48)], self.ra1.at[0], self.ss(5), self.rs(5), p.first(1))
        send(self.own.at[yy, xx, pl.ds(48, 48)], self.ra1.at[1], self.ss(6), self.rs(6), p.first(-1))

    def first(self):
        p = self.p
        wait_bytes(self.ra1.at[0], self.rs(5))
        yy, xx = p.block((p.f + 1) % 4, p.s)
        self.own[yy, xx, 0:48] = (self.own[yy, xx, 0:48].astype(F32) + self.ra1[0].astype(F32)).astype(BF)
        send(self.own.at[yy, xx], self.ra2.at[0], self.ss(7), self.rs(7), p.first(1))
        wait_bytes(self.ra1.at[1], self.rs(6))
        yy, xx = p.block((p.f + 3) % 4, p.s)
        self.own[yy, xx, 48:96] = (self.own[yy, xx, 48:96].astype(F32) + self.ra1[1].astype(F32)).astype(BF)
        send(self.own.at[yy, xx], self.ra2.at[1], self.ss(8), self.rs(8), p.first(-1))

    def beside(self):
        p = self.p
        wait_bytes(self.ra2.at[0], self.rs(7))
        wait_bytes(self.ra2.at[1], self.rs(8))
        yy, xx = p.block(p.f, p.s)
        value = self.own[yy, xx].astype(F32) + self.ra2[0].astype(F32) + self.ra2[1].astype(F32)
        self.zs[...] = jnp.where(p.zlo == 0, value[48:], value[:48]).astype(BF)
        self.keep[...] = jnp.where(p.zlo == 0, value[:48], value[48:])
        send(self.zs, self.zr, self.ss(9), self.rs(9), p.zmate)

    def home(self):
        p = self.p
        wait_bytes(self.zr, self.rs(9))
        value = self.keep[...] + self.zr[...].astype(F32)
        mine = pl.ds(pl.multiple_of(p.core * self.width, 128), self.width)
        self.result[:, mine] = jnp.where(p.core == 0, value[:24], value[24:])
        self.ds[...] = jnp.where(p.core == 0, value[24:], value[:24])
        send(self.ds, self.result.at[:, mine], self.ss(10), self.rs(10), p.partner)

    def finish(self):
        wait_bytes(self.ds, self.rs(10))
        wait_bytes(self.rhs_far, self.ss(0))
        for k in (5, 6):
            wait_bytes(self.ra1.at[0], self.ss(k))
        for k in (7, 8):
            wait_bytes(self.ra2.at[0], self.ss(k))
        wait_bytes(self.zs, self.ss(9))
        wait_bytes(self.ds, self.ss(10))
        for k in (1, 2):
            wait_bytes(self.rb1.at[0], self.ss(k))
        for k in (3, 4):
            wait_bytes(self.rb2.at[0], self.ss(k))


class Total:
    COUNT = 9

    def __init__(self, place, steps, slots, ssem, rsem, index, tensor):
        p = place
        self.steps, self.slots = steps, slots
        self.ss = lambda k: ssem.at[index, k]
        self.rs = lambda k: rsem.at[index, k]
        self.partners = [
            [p.partner], [p.zmate], [p.xy(0, 1), p.xy(0, 2), p.xy(0, 3)], [p.xy(1, 0), p.xy(2, 0), p.xy(3, 0)],
        ]
        if tensor:
            self.partners.append([p.ring(2)])
        self.sent = []
        self.at = 0

    def start(self):
        at = len(self.sent)
        for device in self.partners[self.at]:
            copy = send(self.steps.at[self.at], self.slots.at[at], self.ss(at), self.rs(at), device)
            self.sent.append(copy)
            at += 1
        self.at += 1

    def take(self):
        count = len(self.partners[self.at - 1])
        value = self.steps[self.at - 1]
        for i in range(len(self.sent) - count, len(self.sent)):
            self.sent[i].wait_recv()
            value = value + self.slots[i]
        self.steps[self.at] = value

    def step(self):
        self.take()
        self.start()

    def finish(self):
        for copy in self.sent:
            copy.wait_send()


def bufs(w):
    return [
        pltpu.VMEM((2, 2, 96, w), BF), pltpu.VMEM((2, 4, 96, w), BF),
        pltpu.VMEM((2, 48, w), BF), pltpu.VMEM((2, 96, w), BF), pltpu.VMEM((48, w), BF), pltpu.VMEM((48, w), BF),
        pltpu.VMEM((48, w), F32), pltpu.VMEM((24, w), F32),
    ]


def scan_backward_kernel(
    x_pre, z, gm, xcp, y_low, sums, small, same, segc, segr, chans, heads, bc, cum_in, cum_t, step_in,
    h_mixed, h_cot_t, h_cot_far, h_wo, h_xin,
    o_gz, o_gx, o_vec, o_gbc, o_gdt, o_heads, o_dwo, o_out,
    mixed, cot_t, cot_far, w_o, xin, far_o, own, bufs_o, result, peer_out, relay_out, got_out, own_out,
    s_ssem, s_rsem, c_ssem, c_rsem, l_sem,
    bias, affinity, b_t, c_t, d_aff, d_b, d_c, d_sums, d_last,
):
    c = pl.program_id(0)
    p = Place()
    columns_at = lambda h: mixed.at[:, pl.ds(pl.multiple_of(h * HALF, 128), HALF)]
    so = Scatter(p, cot_t, cot_far, columns_at, far_o, HALF, own, bufs_o, result, s_ssem, s_rsem, 0)
    cross_out = Cross(p, relay_out, c_ssem, c_rsem, 0)
    loads = [
        pltpu.make_async_copy(src, dst, l_sem.at[i])
        for i, (src, dst) in enumerate(((h_mixed, mixed), (h_cot_t, cot_t), (h_cot_far, cot_far), (h_wo, w_o), (h_xin, xin)))
    ]

    @pl.when(c == 0)
    def _():
        for load in loads:
            load.start()
        p.greet()
        loads[0].wait()
        so.give()

    @pl.when(c == 1)
    def _():
        loads[1].wait()
        loads[2].wait()
        so.own_half()

    @pl.when(c == 2)
    def _():
        so.second()
        loads[3].wait()

        @pl.loop(0, 4)
        def _(yy):
            value = dot_nt(mixed[:, 0:HALF], w_o[0, yy].reshape(384, HALF))
            value += dot_nt(mixed[:, HALF:D], w_o[1, yy].reshape(384, HALF))
            cols = pl.ds(pl.multiple_of(yy * 384, 128), 384)
            low, high = value[0:256], value[256:512]
            own_out[:, cols] = jnp.where(p.tz == 0, low, high)
            peer_out[:, cols] = jnp.where(p.tz == 0, high, low).astype(BF)

        cross_out.start(peer_out.at[pl.ds(0, 128)], peer_out.at[pl.ds(128, 128)])

    @pl.when(c == 3)
    def _():
        so.first_far()

    @pl.when(c == 4)
    def _():
        so.first()
        cross_out.forward(lambda t: got_out.at[pl.ds(0, 128)], lambda t: got_out.at[pl.ds(128, 128)])

    @pl.when(c == 5)
    def _():
        so.beside()

    @pl.when(c == 0)
    def _():
        for b in range(2):
            rows = slice(256 * b, 256 * b + 256)
            bias[b] = doc_bias(b, segc, segr, True)
            affinity[b] = fine(dot_nt, bc[rows, 0:128], bc[rows, 128:256])
        b_t[...] = bc[0:256, 0:128].T
        c_t[...] = bc[256:512, 128:256].T
        for ref in (d_aff, d_b, d_c, d_sums, d_last):
            ref[...] = jnp.zeros_like(ref)

    inv = lax.rsqrt(sums[:, 0:1] * (1.0 / 3072) + EPS)
    pull = inv * inv * inv * sums[:, 1:2] * (1.0 / 3072)
    gate = z[...]
    sigma = jax.nn.sigmoid(gate)
    act = gate * sigma
    pre = xcp[...]
    sigma_x = jax.nn.sigmoid(pre)
    xc = pre * sigma_x
    y = y_low[...] + chans[6:7, :] * xc
    gated = y * act
    unit = gated * inv
    gain = chans[5:6, :]
    grad_mixed = gm[...]
    o_vec[5:6, :] = jnp.sum(grad_mixed * unit, axis=0, keepdims=True)
    grad = inv * (grad_mixed * gain) - gated * pull
    gy = grad * act
    o_gz[...] = (grad * y * slope_of(gate, sigma)).astype(BF)
    o_vec[6:7, :] = jnp.sum(gy * xc, axis=0, keepdims=True)
    o_vec[7:8, :] = jnp.zeros((1, CHUNK), F32)
    columns = head_columns(cum_in[...], c)
    cum = on_channels(columns)
    step = on_channels(head_columns(step_in[...], c))
    scaled = step * xc
    x_parts, g_parts = split(scaled), split(gy)
    low, gy_low = x_parts[0], g_parts[0]
    x_swapped, g_swapped = split(swap(scaled)), split(swap(gy))
    alone = apart(gy_low)
    left = [side(packed(x_parts, k, x_swapped, 0, 1), packed(x_parts, k, x_swapped, 0, None)) for k in range(HEADS)]
    right = [side(packed(g_parts, k, g_swapped, 0, 0), packed(g_parts, k, g_swapped, 1, None)) for k in range(HEADS)]
    pieces = []
    for b in range(2):
        base = 256 * b
        rows = slice(base, base + 256)
        parts = []
        spot = jnp.zeros((256, 256), F32)
        for k in range(HEADS):
            gap = cum_t[HEADS * c + k, :, rows] - twice(columns[k][rows], 256)
            decay = jnp.exp2(gap + bias[b])
            parts.append((decay * affinity[b]).astype(BF))
            spot += decay * dot_nt(left[k][rows], right[k][rows])
        d_aff[b] += spot
        pieces.append(dot(side(*parts), below(*[v[rows] for v in alone])))
    linked = same[:, 4:5]
    tail = jnp.exp2(cum[255:256] - cum[0:256]) * linked[0:256]
    sent = tail * scaled[0:256]
    state = fine(dot, b_t[...], sent)
    read = jnp.exp2(cum[256:512]) * linked[256:512] * gy[256:512]
    d_state = fine(dot, c_t[...], read)
    by_state = tail * dot(bc[0:256, 0:128].astype(BF), d_state.astype(BF))
    d_b[0:256, :] += fine(dot_nt, sent, d_state)
    d_c[256:512, :] += fine(dot_nt, read, state)
    low_f = low.astype(F32)
    place = head_of_channel(c)
    pick = (place == 0).astype(F32).astype(BF)
    pick_far = (place == 64).astype(F32).astype(BF)
    ends = jnp.broadcast_to(jnp.sum(low_f[0:256] * by_state, axis=0, keepdims=True), (8, CHUNK))
    d_last[...] += dot(side(*split(ends)), below(pick, pick))
    d_scaled = below(pieces[0], pieces[1]) + below(by_state, jnp.zeros((256, CHUNK), F32))
    moments = side(*split(gy_low.astype(F32) * y_low[...] - low_f * d_scaled), *split(xc * d_scaled))
    d_sums[...] += dot(moments, below(pick, pick, pick_far, pick_far))
    gp = (step * d_scaled + chans[6:7, :] * gy) * slope_of(pre, sigma_x)
    values = x_pre[...].astype(F32)
    summed = chans[3:4, :] * gp
    o_vec[3:4, :] = jnp.sum(gp * values, axis=0, keepdims=True)
    o_vec[4:5, :] = jnp.sum(gp, axis=0, keepdims=True)
    for d in (1, 2, 3):
        moved = pltpu.roll(gp * same[:, d : d + 1], SEQ - d, 0)
        summed = summed + chans[3 - d : 4 - d, :] * moved
        o_vec[3 - d : 4 - d, :] = jnp.sum(moved * values, axis=0, keepdims=True)
    o_gx[...] = summed.astype(BF)

    @pl.when(c == pl.num_programs(0) - 1)
    def _():
        i = lax.broadcasted_iota(jnp.int32, (256, 256), 0)
        j = lax.broadcasted_iota(jnp.int32, (256, 256), 1)
        upper = (j >= i).astype(F32)
        lane = lax.broadcasted_iota(jnp.int32, (256, 128), 1)
        d_sums[255:256, :] += d_last[0:1, :]
        d_step = pltpu.roll(d_sums[...], 64, 1)
        rate = heads[1:2, :]
        raw = small[...] + heads[0:1, :]
        slope = jax.nn.sigmoid(raw)
        bias_sum = jnp.zeros((1, 128), F32)
        rate_sum = jnp.zeros((1, 128), F32)
        for b in range(2):
            rows = slice(256 * b, 256 * b + 256)
            o_gbc[rows, 0:128] = d_b[rows] + fine(dot, d_aff[b], bc[rows, 128:256])
            o_gbc[rows, 128:256] = d_c[rows] + fine(dot_tn, d_aff[b], bc[rows, 0:128])
            d_log = jnp.dot(upper, d_sums[rows], precision=HIGH, preferred_element_type=F32)
            grad_raw = (d_step[rows] + rate * d_log) * slope[rows]
            grad_raw = jnp.where(lane < 24, grad_raw, 0.0)
            o_gdt[rows] = grad_raw.astype(BF)
            bias_sum += jnp.sum(grad_raw, axis=0, keepdims=True)
            rate_sum += jnp.sum(d_log * step_in[rows] * rate, axis=0, keepdims=True)
        o_heads[...] = jnp.zeros_like(o_heads)
        o_heads[0:1, :] = bias_sum
        o_heads[1:2, :] = rate_sum
        so.home()
        cross_out.ready()
        cross_out.release()
        loads[4].wait()
        for i in range(8):
            part = slice(32 * i, 32 * i + 32)
            peer_out[part, :] = (xin[part, :].astype(F32) + own_out[part, :] + got_out[part, :].astype(F32)).astype(BF)
        so.finish()
        cross_out.finish()
        stores = [pltpu.make_async_copy(result, o_dwo, l_sem.at[5]), pltpu.make_async_copy(peer_out, o_out, l_sem.at[6])]
        for copy in stores:
            copy.start()
        for copy in stores:
            copy.wait()


def block_spec(shape):
    if len(shape) == 3:
        return pl.BlockSpec(shape, lambda c: (0, 0, 0))
    rows, width = shape
    if width == SEQ and rows == SEQ:
        return pl.BlockSpec((rows, 128), lambda c: (0, 1))
    if width == D:
        return pl.BlockSpec((rows, CHUNK), lambda c: (0, c))
    return pl.BlockSpec((rows, width), lambda c: (0, 0))


def scan_backward(args, far):
    sds = jax.ShapeDtypeStruct
    outs = [
        sds((SEQ, D), BF), sds((SEQ, D), BF), sds((8, D), F32), sds((SEQ, 256), F32), sds((SEQ, 128), BF), sds((8, 128), F32),
    ]
    far_outs = [sds((24, D), F32), sds((256, D), BF)]
    half = pltpu.VMEM((4, 4, 96, HALF), BF)
    wide = lambda n, t: pltpu.VMEM((n, D), t)
    square = pltpu.VMEM((2, 256, 256), F32)
    rows = pltpu.VMEM((SEQ, 128), F32)
    scratch = [
        wide(SEQ, BF), pltpu.VMEM((D, SEQ), BF), pltpu.VMEM((D, SEQ), BF), pltpu.VMEM((2, 4, 4, 96, HALF), BF), wide(256, BF),
        pltpu.VMEM((SEQ, HALF), BF), half, bufs(HALF),
        wide(24, F32), wide(256, BF), pltpu.VMEM((2, 128, D), BF), wide(256, BF), wide(256, F32),
        pltpu.SemaphoreType.DMA((1, Scatter.COUNT)), pltpu.SemaphoreType.DMA((1, Scatter.COUNT)),
        pltpu.SemaphoreType.DMA((1, 4)), pltpu.SemaphoreType.DMA((1, 4)), pltpu.SemaphoreType.DMA((7,)),
        square, square, pltpu.VMEM((128, 256), F32), pltpu.VMEM((128, 256), F32), square, rows, rows, rows,
        pltpu.VMEM((8, 128), F32),
    ]
    any_space = pl.BlockSpec(memory_space=pl.ANY)
    return pl.pallas_call(
        scan_backward_kernel,
        grid=(D // CHUNK,),
        out_shape=outs + far_outs,
        in_specs=[block_spec(a.shape) for a in args] + [any_space] * len(far),
        out_specs=[block_spec(o.shape) for o in outs] + [any_space] * len(far_outs),
        scratch_shapes=scratch,
        compiler_params=pltpu.CompilerParams(collective_id=2, has_side_effects=True, vmem_limit_bytes=62 * 1024 * 1024),
        cost_estimate=pl.CostEstimate(flops=8_000_000_000, bytes_accessed=30_000_000, transcendentals=5_000_000),
    )(*args, *far)


def back_kernel(
    h_normed_t, h_normed_far, h_gz, h_gx, h_gdt, h_gbc, h_bcc, h_small, h_same, h_taps, h_vec, h_heads, h_xin, h_cin, h_aux,
    h_ws, h_wx, h_wz,
    o_dx, o_dwx, o_dwz, o_dbc, o_ddt, o_cxw, o_cxb, o_gate, o_cbw, o_cbb, o_dtb, o_alog, o_skip, o_gain,
    normed_t, normed_far, gz, gx, gdt, gbc, bcc, bcp, same, taps, vec, heads, xin, cin, aux, w_s, w_a, w_b,
    gs, far_s, far_x, far_z, own_s, own_x, own_z,
    bufs_s, bufs_x, bufs_z, res_s, res_x, res_z,
    peer_g, relay_g, got_g, own_g, relay_bc, got_bc,
    vec_slots, gain_steps, gain_slots,
    s_ssem, s_rsem, c_ssem, c_rsem, t_ssem, t_rsem, l_sem,
):
    p = Place()
    pairs = [
        (h_gbc, gbc), (h_gz, gz), (h_gx, gx), (h_gdt, gdt), (h_ws, w_s), (h_wz, w_b), (h_wx, w_a), (h_normed_t, normed_t),
        (h_normed_far, normed_far), (h_bcc, bcc), (h_small.at[:, pl.ds(0, 128)], bcp.at[:, pl.ds(0, 128)]),
        (h_small.at[:, pl.ds(256, 128)], bcp.at[:, pl.ds(128, 128)]), (h_same, same), (h_taps, taps), (h_vec, vec.at[0]),
        (h_heads, heads), (h_xin, xin), (h_cin, cin), (h_aux, aux),
    ]
    waits = {}
    for i, (src, dst) in enumerate(pairs):
        copy = pltpu.make_async_copy(src, dst, l_sem.at[i])
        copy.start()
        waits[i] = copy
    index = {"gbc": 0, "gz": 1, "gx": 2, "gdt": 3, "ws": 4, "wz": 5, "wx": 6, "normed_t": 7, "normed_far": 8, "bcc": 9, "bcp": 10,
             "bcp_far": 11, "same": 12, "taps": 13, "vec": 14, "heads": 15, "xin": 16, "cin": 17, "aux": 18}

    def need(*names):
        for name in names:
            waits[index[name]].wait()

    p.greet(more=True)

    def columns(ref):
        return lambda h: ref.at[:, pl.ds(pl.multiple_of(h * HALF, 128), HALF)]

    sz = Scatter(p, normed_t, normed_far, columns(gz), far_z, HALF, own_z, bufs_z, res_z, s_ssem, s_rsem, 0)
    sx = Scatter(p, normed_t, normed_far, columns(gx), far_x, HALF, own_x, bufs_x, res_x, s_ssem, s_rsem, 1)
    sb = Scatter(p, normed_t, normed_far, lambda h: gs.at[h], far_s, 256, own_s, bufs_s, res_s, s_ssem, s_rsem, 2)
    cross_bc = Cross(p, relay_bc, c_ssem, c_rsem, 0)
    cross_g = Cross(p, relay_g, c_ssem, c_rsem, 1)
    total_vec = Total(p, vec, vec_slots, t_ssem, t_rsem, 0, False)
    total_gain = Total(p, gain_steps, gain_slots, t_ssem, t_rsem, 1, True)
    mine = pl.ds(pl.multiple_of(p.tz * 256, 256), 256)

    need("gbc")
    cross_bc.start(gbc.at[pl.ds(0, 256)], gbc.at[pl.ds(256, 256)])
    need("gz")
    sz.give()
    need("gx")
    sx.give()
    need("gdt", "wx", "wz", "ws")
    def share_out(value, yy, own, peer):
        cols = pl.ds(pl.multiple_of(yy * 384, 128), 384)
        low, high = value[0:256], value[256:512]
        own[:, cols] = jnp.where(p.tz == 0, low, high)
        peer[:, cols] = jnp.where(p.tz == 0, high, low).astype(BF)

    @pl.loop(0, 4)
    def _(yy):
        value = dot_nt(gdt[...], w_s[0, yy, :, :, 128:256].reshape(384, 128))
        for h in range(2):
            cols = slice(HALF * h, HALF * h + HALF)
            value += dot_nt(gz[:, cols], w_b[h, yy].reshape(384, HALF))
            value += dot_nt(gx[:, cols], w_a[h, yy].reshape(384, HALF))
        share_out(value, yy, own_g, peer_g)

    cross_g.start(peer_g.at[pl.ds(0, 128)], peer_g.at[pl.ds(128, 128)])


    need("normed_t", "normed_far")
    sz.own_half()
    cross_bc.forward(lambda t: got_bc.at[pl.ds(0, 256)], lambda t: got_bc.at[pl.ds(256, 256)])
    sx.own_half()
    cross_g.forward(lambda t: got_g.at[pl.ds(0, 128)], lambda t: got_g.at[pl.ds(128, 128)])
    sz.second()
    cross_bc.ready()
    need("heads", "bcp_far", "bcc", "bcp", "same", "taps", "vec")
    pre_bc = bcc[...]
    sigma = sig(pre_bc)
    slope = sigma * (1.0 + pre_bc * (1.0 - sigma))
    before = (gbc[...] + got_bc[...]) * slope
    inner = taps[3:4, :] * before
    vec[0, 7:8, 1024:1280] = jnp.sum(before, axis=0, keepdims=True)
    vec[0, 7:8, 1280:1408] = heads[0:1, :]
    vec[0, 7:8, 1408:1536] = heads[1:2, :]
    vec[0, 7:8, 768:1024] = jnp.sum(before * bcp[...], axis=0, keepdims=True)
    for d in (1, 2, 3):
        moved = pltpu.roll(before * same[:, d : d + 1], SEQ - d, 0)
        inner += taps[3 - d : 4 - d, :] * moved
        vec[0, 7:8, 256 * (3 - d) : 256 * (4 - d)] = jnp.sum(moved * bcp[...], axis=0, keepdims=True)
    gs[0, :, 0:128] = inner[:, :128].astype(BF)
    gs[1, :, 0:128] = inner[:, 128:].astype(BF)
    gs[0, :, 128:256] = gdt[...]
    gs[1, :, 128:256] = jnp.zeros((SEQ, 128), BF)
    sb.give()
    total_vec.start()
    @pl.loop(0, 4)
    def _(yy):
        cols = pl.ds(pl.multiple_of(yy * 384, 128), 384)
        weights = side(w_s[0, yy, :, :, 0:128].reshape(384, 128), w_s[1, yy, :, :, 0:128].reshape(384, 128))
        own_g[:, cols] += dot_nt(side(gs[0, mine, 0:128], gs[1, mine, 0:128]), weights)

    sx.second()
    sb.own_half()
    cross_g.ready()
    need("xin", "cin", "aux")
    gain = aux[0:1, :]
    sums = jnp.zeros((8, D), F32)
    for i in range(16):
        part = slice(16 * i, 16 * i + 16)
        rows = xin[part, :].astype(F32)
        inv = lax.rsqrt(jnp.mean(rows * rows, axis=-1, keepdims=True) + EPS)
        unit = rows * inv
        grad = own_g[part, :] + got_g[part, :].astype(F32)
        weighted = grad * unit
        sums += weighted.reshape(2, 8, D).sum(axis=0)
        mean = jnp.mean(weighted * gain, axis=-1, keepdims=True)
        own_g[part, :] = inv * (grad * gain - unit * mean) + cin[part, :].astype(F32)
    store_dx = pltpu.make_async_copy(own_g, o_dx, l_sem.at[len(pairs)])
    store_dx.start()
    gain_steps[0] = jnp.broadcast_to(jnp.sum(sums, axis=0, keepdims=True), (8, D))
    total_gain.start()
    sz.first_far()
    total_vec.step()
    sx.first_far()
    sz.first()
    total_gain.step()
    sb.second()
    total_vec.step()
    sx.first()
    sz.beside()
    total_gain.step()
    sb.first_far()
    total_vec.step()
    sz.home()
    sx.beside()
    total_gain.step()
    sb.first()
    total_vec.take()
    sx.home()
    total_gain.step()
    sb.beside()
    sb.home()
    total_gain.take()
    done = vec[4]
    o_cxw[...] = done[0:4]
    o_cxb[...] = done[4:5]
    o_gate[...] = done[5:6]
    channel = lax.broadcasted_iota(jnp.int32, (D, 128), 0)
    head = lax.broadcasted_iota(jnp.int32, (D, 128), 1)
    pick = (channel // 64 == head).astype(F32).astype(BF)
    skips = dot(side(*split(jnp.broadcast_to(done[6:7], (8, D)))), below(pick, pick))
    o_skip[...] = skips[0:1, 0:24]
    o_dtb[...] = done[7:8, 1280:1304]
    o_alog[...] = done[7:8, 1408:1432]
    rank = p.dp * 2 + p.tz
    for k in range(5):
        moved = pltpu.roll(done[:, 256 * k : 256 * k + 256], (256 - 2 * rank) % 256, 1)
        if k < 4:
            o_cbw[k : k + 1, :] = moved[7:8, 0:2]
        else:
            o_cbb[...] = moved[7:8, 0:2]
    o_gain[...] = pltpu.roll(gain_steps[5], (D - 12 * rank) % D, 1)[0:1, 0:12]
    results = [(res_x, o_dwx), (res_z, o_dwz)]
    for scatter in (sz, sx, sb):
        scatter.finish()
    both = side(res_s[:, 0:128], res_s[:, 256:384])
    o_dbc[...] = jnp.where(p.tz == 0, both, pltpu.roll(both, 12, 0))[0:12]
    o_ddt[...] = res_s[:, 128:152]
    stores = []
    for i, (src, dst) in enumerate(results):
        copy = pltpu.make_async_copy(src, dst, l_sem.at[len(pairs) + 1 + i])
        copy.start()
        stores.append(copy)
    cross_bc.release()
    cross_g.release()
    for cross in (cross_bc, cross_g):
        cross.finish()
    total_vec.finish()
    total_gain.finish()
    store_dx.wait()
    for copy in stores:
        copy.wait()


def back(args):
    any_space = pl.BlockSpec(memory_space=pl.ANY)
    sds = jax.ShapeDtypeStruct
    vmem = pl.BlockSpec(memory_space=pltpu.VMEM)
    piece = sds((24, D), F32)
    small = [(12, 256), (24, 24), (4, D), (1, D), (1, D), (4, 2), (1, 2), (1, 24), (1, 24), (1, 24), (1, 12)]
    outs = [sds((256, D), F32), piece, piece] + [sds(s, F32) for s in small]

    half = lambda w: pltpu.VMEM((4, 4, 96, w), BF)
    wide = pltpu.VMEM((2, 4, 4, 96, HALF), BF)
    rows = lambda n, t: pltpu.VMEM((n, D), t)
    scratch = [
        pltpu.VMEM((D, SEQ), BF), pltpu.VMEM((D, SEQ), BF), rows(SEQ, BF), rows(SEQ, BF),
        pltpu.VMEM((SEQ, 128), BF), pltpu.VMEM((SEQ, 256), F32), pltpu.VMEM((SEQ, 256), F32), pltpu.VMEM((SEQ, 256), F32),
        pltpu.VMEM((SEQ, 128), F32), pltpu.VMEM((8, 256), F32), pltpu.VMEM((5, 8, D), F32), pltpu.VMEM((8, 128), F32),
        rows(256, BF), rows(256, BF), rows(8, F32), pltpu.VMEM((2, 4, 4, 96, 256), BF), wide, wide,
        pltpu.VMEM((2, SEQ, 256), BF), pltpu.VMEM((SEQ, 256), BF), pltpu.VMEM((SEQ, HALF), BF), pltpu.VMEM((SEQ, HALF), BF),
        half(256), half(HALF), half(HALF),
        bufs(256), bufs(HALF), bufs(HALF),
        pltpu.VMEM((24, 512), F32), rows(24, F32), rows(24, F32),
        rows(256, BF), pltpu.VMEM((2, 128, D), BF), rows(256, BF), rows(256, F32),
        pltpu.VMEM((2, 256, 256), F32), pltpu.VMEM((SEQ, 256), F32),
        pltpu.VMEM((8, 8, D), F32), pltpu.VMEM((6, 8, D), F32), pltpu.VMEM((9, 8, D), F32),
        pltpu.SemaphoreType.DMA((3, Scatter.COUNT)), pltpu.SemaphoreType.DMA((3, Scatter.COUNT)),
        pltpu.SemaphoreType.DMA((2, 4)), pltpu.SemaphoreType.DMA((2, 4)),
        pltpu.SemaphoreType.DMA((2, Total.COUNT)), pltpu.SemaphoreType.DMA((2, Total.COUNT)),
        pltpu.SemaphoreType.DMA((32,)),
    ]
    return pl.pallas_call(
        back_kernel,
        out_shape=outs,
        in_specs=[any_space] * len(args),
        out_specs=[any_space] * 3 + [vmem] * len(small),
        scratch_shapes=scratch,
        compiler_params=pltpu.CompilerParams(collective_id=1, has_side_effects=True, vmem_limit_bytes=63 * 1024 * 1024),
        cost_estimate=pl.CostEstimate(flops=2 * SEQ * D * 10240, bytes_accessed=50_000_000, transcendentals=0),
    )(*args)


def settle_kernel(count, *refs):
    for i in range(count):
        refs[count + i][...] = refs[i][...]


def settle(results):
    specs = [pl.BlockSpec(memory_space=pltpu.VMEM)] * len(results)
    return pl.pallas_call(
        functools.partial(settle_kernel, len(results)),
        out_shape=[jax.ShapeDtypeStruct(v.shape, v.dtype) for v in results],
        in_specs=specs,
        out_specs=specs,
        compiler_params=pltpu.CompilerParams(vmem_limit_bytes=62 * 1024 * 1024),
    )(*results)


def per_device(
    block_input, cotangent, seg_ids, norm_gain, w_z, w_x, w_bc, w_dt, conv_x_w, conv_x_b, conv_bc_w, conv_bc_b,
    dt_bias, a_log, d_skip, gate_gain, w_out,
):
    tz = lax.axis_index("tensor")
    first = (tz == 0).astype(F32)
    conv = jnp.pad(conv_bc_w.astype(F32).T, ((0, 0), (0, 1))) + jnp.pad(conv_bc_b.astype(F32)[:, None], ((0, 0), (4, 0)))
    own = jnp.pad(w_bc.astype(F32), ((0, 0), (0, 256)))
    own = own + jnp.pad(norm_gain.astype(F32)[:, None], ((0, 0), (256, 255))) + jnp.pad(conv, ((0, 10), (257, 250)))
    tiny = jnp.pad(own * first, ((0, 12), (0, 0))) + jnp.pad(own * (1.0 - first), ((12, 0), (0, 0)))
    tiny = tiny + jnp.pad(w_dt.astype(F32), ((0, 0), (384, 104)))
    segr = jnp.broadcast_to(seg_ids.astype(F32)[None, :], (8, SEQ))
    put = lambda v, row, lane: jnp.pad(v.astype(F32)[None], ((row, 7 - row), (lane, D - lane - v.shape[0])))
    chan_in = jnp.pad(conv_x_w.astype(F32), ((0, 4), (0, 0))) + put(conv_x_b, 4, 0) + put(gate_gain, 5, 0)
    chan_in = chan_in + put(dt_bias, 6, 0) + put(a_log, 6, 128) + put(d_skip, 6, 256)
    (
        normed_t, cot_t, x_pre, z_part, grad_mixed, small, aux, ws, wx, wz, wo,
        xcp, y_low, sums, bcc, bc, cum, cum_t, step, same, segc, taps, chans, heads, mixed, normed_far, cot_far,
    ) = front((w_x, w_z, w_out.T, tiny, segr, chan_in, block_input, cotangent))
    gz, gx, vec, gbc, gdt, d_heads, dwo, out = scan_backward(
        (x_pre, z_part, grad_mixed, xcp, y_low, sums, small, same, segc, segr, chans, heads, bc, cum, cum_t, step),
        (mixed, cot_t, cot_far, wo, block_input),
    )
    results = back(
        (normed_t, normed_far, gz, gx, gdt, gbc, bcc, small, same, taps, vec, d_heads, block_input, cotangent, aux, ws, wx, wz)
    )
    out, dwo, d_x, dwx, dwz, d_bc, d_dt, cxw, cxb, d_gate, cbw, cbb, d_bias, d_rate, d_skips, gain = settle([out, dwo, *results])
    flat = lambda v: v.reshape(v.shape[1])
    return (
        out, d_x, flat(gain), dwz, dwx, d_bc, d_dt, cxw, flat(cxb), cbw, flat(cbb), flat(d_bias), flat(d_rate), flat(d_skips),
        flat(d_gate), dwo.T,
    )


def solution(mesh):
    both = ("dp", "tensor")
    in_specs = (
        P(both, None), P(both, None), P("dp"), P(both), P("dp", "tensor"), P("dp", "tensor"), P(both, None), P("dp", "tensor"),
        P(None, "tensor"), P("tensor"), P(None, both), P(both), P("tensor"), P("tensor"), P("tensor"), P("tensor"),
        P("tensor", "dp"),
    )
    out_specs = (
        P(both, None), P(both, None), P(both), P("dp", "tensor"), P("dp", "tensor"), P(both, None), P("dp", "tensor"),
        P(None, "tensor"), P("tensor"), P(None, both), P(both), P("tensor"), P("tensor"), P("tensor"), P("tensor"),
        P("tensor", "dp"),
    )
    return jax.shard_map(per_device, mesh=mesh, in_specs=in_specs, out_specs=out_specs, check_vma=False)
```

time: 2390 us -> 233 us (0.10)
  blocking collectives: 1490 us -> 0 us
  waiting for transfers between devices: 416 us -> 0 us
  Pallas kernels: 0 us -> 218 us
  matrix products: 165 us -> 0 us
  local copies, waits for them, and re-layouts: 123 us -> 4.83 us
  starting transfers between devices: 91.9 us -> 0 us
  other arithmetic: 70.1 us -> 7.52 us
    all_gather x3 -> x0, blocking collectives: 711 us -> none  [the longest x1 318 us: per_device(): lax.all_gather(w_bc, ('dp', 'tensor'), axis=0, tiled=True)]
    unnamed x3 -> x0, blocking collectives: 493 us -> none
    reduce_scatter x5 -> x0, waiting for transfers between devices: 412 us -> none  [the longest x1 300 us: per_device(): lax.psum_scatter(grad_w_z, 'dp', scatter_dimension=0, tiled=True)]
    psum x3 -> x0, blocking collectives: 290 us -> none  [the longest x1 276 us: per_device(): lax.psum((grad_kern_x, grad_offset_x, grad_dtbias, grad_alog, grad_dskip,...]
    pallas_call x0 -> x4, Pallas kernels: none -> 218 us  [the longest x1 102 us: front(): pl.pallas_call(front_kernel, out_shape=[jax.ShapeDtypeStruct(*t) for t in...]
    dot_general x26 -> x0, matrix products: 161 us -> none  [the longest x3 48.1 us: state_space(): within = jnp.einsum('chij,cjhp->cihp', mixing, values, precision=highest)]
    unnamed x33 -> x0, starting transfers between devices: 91.4 us -> none
    unnamed x292 -> x1, local copies, waits for them, and re-layouts: 36.9 us -> 1.32 us
  transfers between devices with their start and end apart: 44 -> 0, of which waited for: 3 -> 0; matrix products, arithmetic and copies ran while one was open for 24% -> 0% of each run, Pallas kernels for 0% -> 0%
where the time goes in v1:
time: 233 us; the launch traced here: 231 us
  Pallas kernels  218 us (94%)
  other arithmetic  7.52 us (3%)
  local copies, waits for them, and re-layouts  4.83 us (2%)
    pallas_call x1, Pallas kernels, front(): pl.pallas_call(front_kernel, out_shape=[jax.ShapeDtypeStruct(*t) for t in...  102 us
    pallas_call x1, Pallas kernels, back(): pl.pallas_call(back_kernel, out_shape=outs, in_specs=[any_space] * len(ar...  67.2 us
    pallas_call x1, Pallas kernels, scan_backward(): pl.pallas_call(scan_backward_kernel, grid=(D // CHUNK,), out_shape=outs +...  45.2 us

profile of v1, /device:TPU:0, one launch (start us, length us, event | category | flops | bytes accessed | tf_op | source)
XLA Modules:
  0.0 231.5 jit_solution(2161308908035525354)
XLA Ops:
  0.7 0.8 copy.34
  1.4 0.7 convert_add_fusion.2
  2.1 0.7 convert_element_type.29
  2.8 0.7 copy.33
  3.6 0.7 broadcast_in_dim.37
  4.3 0.7 broadcast_in_dim.38
  5.0 0.6 broadcast_in_dim.36.segr
  5.6 1.4 convert_add_fusion.chan_in
  7.0 0.8 fusion.1
  7.7 1.3 convert_add_fusion.1.tiny
  9.1 102.5 %shard_map.288 = (bf16[1536,512]{1,0:T(8,128)(2,1)}, bf16[1536,512]{1,0:T(8,128)(2,1)}, bf16[512,1536]{1,0:T(8,128)(2,1)}, f32[512,1536]{1,0:T(8,128)}, f32[512,...) custom-call(bf16[24,1536]{1,0:T(8,128)(2,1)} %wx_in.1, ...), custom_call_target="tpu_custom_call" | custom-call | flops 9437184000 | bytes 60000000 | tf_op jit(solution)/shard_map/pallas_call | solution.py:613
  111.6 45.2 %shard_map.289 = (bf16[512,1536]{1,0:T(8,128)(2,1)}, bf16[512,1536]{1,0:T(8,128)(2,1)}, f32[8,1536]{1,0:T(8,128)}, f32[512,256]{1,0:T(8,128)}, bf16[512,128]{1,0...) custom-call(bf16[512,1536]{1,0:T(8,128)(2,1)} %get-tuple-element.81.x_pre, ...), custom_call_target="tpu_custom_call" | custom-call | flops 8000000000 | bytes 30000000 | tf_op jit(solution)/shard_map/pallas_call | solution.py:1003
  156.8 67.2 %shard_map.290 = (f32[256,1536]{1,0:T(8,128)}, f32[24,1536]{1,0:T(8,128)}, f32[24,1536]{1,0:T(8,128)}, f32[12,256]{1,0:T(8,128)}, f32[24,24]{1,0:T(8,128)}, /*in...) custom-call(bf16[1536,512]{1,0:T(8,128)(2,1)} %get-tuple-element.102, ...), custom_call_target="tpu_custom_call" | custom-call | flops 16106127360 | bytes 50000000 | tf_op jit(solution)/shard_map/pallas_call | solution.py:1228
  224.0 3.5 %shard_map.291 = (bf16[256,1536]{1,0:T(8,128)(2,1)}, f32[24,1536]{1,0:T(8,128)}, f32[256,1536]{1,0:T(8,128)}, f32[24,1536]{1,0:T(8,128)}, f32[24,1536]{1,0:T(8,1...) custom-call(bf16[256,1536]{1,0:T(8,128)(2,1)} %get-tuple-element.100, ...), custom_call_target="tpu_custom_call" | custom-call | tf_op jit(solution)/shard_map/pallas_call | solution.py:1246
  227.5 1.3 copy.35
  228.9 1.3 reduce
  230.2 1.3 reduce.1
